TPU v7x, 32 devices: a whole 2x2x4 slice. The times are simulated.
32 devices in a mesh: dp: 16 (over z, y, core), feat: 2 (over x).
Axes of the slice: x: 2, y: 2, z: 4, core: 2. Of those that a mesh axis runs over, the one named last changes fastest.
Arguments:
- table: bfloat16 [2048, 3584], P('dp', 'feat'), may hold values from -64 to 64
- text: bfloat16 [2048, 3584], P('dp', 'feat'), may hold values from -64 to 64
- table_proj: bfloat16 [3584, 4096], P(None, 'feat'), may hold values from -1 to 1
- text_proj: bfloat16 [3584, 4096], P(None, 'feat'), may hold values from -1 to 1
Outputs:
- grad_table: float32 [2048, 3584], P('dp', 'feat')
- grad_text: float32 [2048, 3584], P('dp', 'feat')
- loss_mean: float32 [1], replicated
All inputs are finite; a program needn't handle non-finite values.
Results may differ from a plain program's by a relative error of at most 0.0044.
Values may be sent and summed in bfloat16 or wider, within the bound.
No kernel may reach another device: no remote copies, remote signals or barrier semaphores. Data moves between devices by JAX's collectives and lax.ppermute only.
A program may use at most 128 MiB of HBM per device.

v0:
```python
import jax
import jax.numpy as jnp
from jax import lax
from jax.sharding import Mesh
from jax.sharding import PartitionSpec as P

OFF_WEIGHT = 0.1
EPS = 1e-05
Z_CHIPS = 4
F32 = jnp.float32
BF16 = jnp.bfloat16


def dot(a, b, dims):
    return lax.dot_general(a, b, (dims, ((), ())), preferred_element_type=F32)


def shift(x, axis, step):
    size = lax.axis_size(axis)
    return lax.ppermute(x, axis, [(i, (i + step) % size) for i in range(size)])


def flip(x, axis, bit=1):
    size = lax.axis_size(axis)
    return lax.ppermute(x, axis, [(i, i ^ bit) for i in range(size)])


def cube_sum(x, *axes):
    for axis in axes:
        bit = 1
        while bit < lax.axis_size(axis):
            x = x + flip(x, axis, bit)
            bit *= 2
    return x


def own_block(x, index, count, axis):
    size = x.shape[axis] // count
    return lax.dynamic_slice_in_dim(x, index * size, size, axis)


def both_cores(x):
    got = flip(x, "core")
    first = lax.axis_index("core") == 0
    return jnp.where(first, jnp.concatenate([x, got], 0), jnp.concatenate([got, x], 0))


def add_cores(x):
    core = lax.axis_index("core")
    return own_block(x, core, 2, 0) + flip(own_block(x, 1 - core, 2, 0), "core")


def weight_blocks(proj):
    num_feat = lax.axis_size("feat")
    feat = lax.axis_index("feat")
    cols = own_block(proj, lax.axis_index("core"), 2, 1)
    return [own_block(cols, (feat - step) % num_feat, num_feat, 0) for step in range(num_feat)]


def swap_feat(x):
    return [shift(x, "feat", step) for step in range(1, lax.axis_size("feat"))]


def project(mine, others, weights):
    z = dot(both_cores(mine), weights[0], ((1,), (0,)))
    for other, weight in zip(others, weights[1:]):
        z = z + dot(both_cores(other), weight, ((1,), (0,)))
    return z


def normalize(z, pairs):
    sums = cube_sum(jnp.stack([jnp.sum(z, axis=0), jnp.sum(z * z, axis=0)]), "z", "y")
    center = sums[0] / pairs
    spread = sums[1] / pairs - center * center
    inverse = lax.rsqrt(spread + EPS)
    return (z - center) * inverse, inverse


def gather_rows(own):
    z = lax.axis_index("z")
    end = (z == 0) | (z == Z_CHIPS - 1)
    half = own.shape[0] // 2
    near = flip(own, "z")
    mid = lax.ppermute(own, "z", [(1, 2), (2, 1)])
    far_in = lax.ppermute(near, "z", [(1, 2), (2, 1)])
    far_end = lax.ppermute(mid, "z", [(1, 0), (2, 3)])
    far = jnp.where(end, far_end, far_in)
    last_end = lax.ppermute(far_in, "z", [(1, 0), (2, 3)])
    last = jnp.where(end, last_end, mid)
    early, late = [own, near, far], [last]
    for step in range(1, lax.axis_size("y")):
        y_own = shift(own, "y", step)
        y_near = [shift(near[:half], "y", step), flip(y_own[half:], "z")]
        early += [y_own, *y_near, shift(far, "y", step)]
        late += [shift(last, "y", step)]
    return jnp.concatenate(early, 0), jnp.concatenate(late, 0)


def gram_rows(half, rows):
    mine = add_cores(dot(half, rows, ((1,), (1,))))
    sent = mine.astype(BF16)
    for other in swap_feat(sent):
        mine = mine + other.astype(F32)
    return both_cores(mine.astype(BF16))


def backward(d, normed, inverse, pairs):
    sums = jnp.stack([jnp.sum(d, axis=0), jnp.sum(d * normed, axis=0)])
    mean, tilt = cube_sum(sums, "z", "y") / pairs
    return (inverse * (d - mean - normed * tilt)).astype(BF16), tilt


def embed_grad(back, weights):
    num_feat = lax.axis_size("feat")
    others = []
    for step in range(1, num_feat):
        part = add_cores(dot(back, weights[step], ((1,), (1,))))
        others.append(shift(part.astype(BF16), "feat", num_feat - step))
    grad = add_cores(dot(back, weights[0], ((1,), (1,))))
    for other in others:
        grad = grad + other.astype(F32)
    return grad


def body(table, text, table_proj, text_proj):
    pairs = table.shape[0] * 2 * lax.axis_size("z") * lax.axis_size("y")
    features = table_proj.shape[1] * lax.axis_size("feat")
    table_weights = weight_blocks(table_proj)
    text_weights = weight_blocks(text_proj)

    others_table = swap_feat(table)
    text, others_table = lax.optimization_barrier((text, others_table))
    others_text = swap_feat(text)

    normed_table, inverse_table = normalize(project(table, others_table, table_weights), pairs)
    half_table = normed_table.astype(BF16)
    all_table = gather_rows(half_table)
    normed_text, inverse_text = normalize(project(text, others_text, text_weights), pairs)
    half_text = normed_text.astype(BF16)
    all_text = gather_rows(half_text)

    gram_table = [gram_rows(half_table, rows) for rows in all_table]
    gram_text = [gram_rows(half_text, rows) for rows in all_text]

    diag = 0.0
    for rows_table, rows_text in zip(all_table, all_text):
        diag = diag + jnp.sum(rows_table.astype(F32) * rows_text.astype(F32), axis=0)
    diag = diag / pairs
    diag_weight = (diag - 1.0).astype(BF16).astype(F32) - OFF_WEIGHT * diag

    off_text = 0.0
    for gram, rows in zip(gram_table, all_text):
        off_text = off_text + dot(gram, rows, ((1,), (0,)))
    d_text = (OFF_WEIGHT / pairs) * off_text + half_table.astype(F32) * diag_weight
    back_text, _ = backward(d_text, normed_text, inverse_text, pairs)
    grad_text = embed_grad(back_text, text_weights)

    off_table = 0.0
    for gram, rows in zip(gram_text, all_table):
        off_table = off_table + dot(gram, rows, ((1,), (0,)))
    d_table = (OFF_WEIGHT / pairs) * off_table + half_text.astype(F32) * diag_weight
    back_table, tilt_table = backward(d_table, normed_table, inverse_table, pairs)
    grad_table = embed_grad(back_table, table_weights)

    squares = tilt_table - diag_weight * diag
    terms = (1.0 - diag) * (1.0 - diag) - OFF_WEIGHT * diag * diag + squares
    loss_total = cube_sum(jnp.sum(terms).reshape(1), "core", "feat")
    return grad_table, grad_text, loss_total / features


def solution(mesh):
    devices = mesh.devices
    split = Mesh(
        devices.reshape(Z_CHIPS, devices.shape[0] // (2 * Z_CHIPS), 2, devices.shape[1]),
        ("z", "y", "core", "feat"),
    )
    rows = ("z", "y", "core")
    placed = (P(rows, "feat"), P(rows, "feat"), P(None, "feat"), P(None, "feat"))
    return jax.shard_map(
        body,
        mesh=split,
        in_specs=placed,
        out_specs=(P(rows, "feat"), P(rows, "feat"), P()),
        check_vma=False,
    )
```

profile of v0, /device:TPU:0, one launch (start us, length us, event | category | flops | bytes accessed | tf_op | source)
XLA Modules:
  0.0 219.9 jit_solution(260779789007879296)
XLA Ops:
  0.6 3.0 %collective-permute-start.1 = (bf16[128,1792]{1,0:T(8,128)(2,1)}, bf16[128,1792]{1,0:T(8,128)(2,1)S(1)}, u32[]{:S(2)}, u32[]{:S(2)}) collective-permute-start(bf16[128,1792]{1,0:T(8,128)(2,1)} %param.4), channel_id=1, source_target_pairs={{0,1},{1,0},{2,3},{3,2},{4,5},{5,4},{6,7},{7,6},{8,9},{9,8},{10,11... | collective-permute-start | bytes 1376264 | tf_op jit(solution)/shard_map/ppermute | solution.py:20
  3.6 10.7 %collective-permute-done.1 = bf16[128,1792]{1,0:T(8,128)(2,1)S(1)} collective-permute-done((bf16[128,1792]{1,0:T(8,128)(2,1)}, bf16[128,1792]{1,0:T(8,128)(2,1)S(1)}, u32[]{:S(2)}, u32[]{:S(2)}) %collective-permute-start.1) | collective-permute-done | bytes 458784 | tf_op jit(solution)/shard_map/ppermute | solution.py:20
  16.8 4.5 %fusion.10 = f32[256,1024]{1,0:T(8,128)S(1)} fusion(bf16[3584,2048]{1,0:T(8,128)(2,1)} %param.6, s32[]{:T(128)S(6)} %select_n.127, s32[]{:T(128)S(6)} %select_n.123, bf16[128,1792]{1,0:T(8,128)(2,1)S(1)} %collective-permute-done.2, bf16[128,1792]{1,0:T(8,128)(2,1)S(1)} %collective-permute-done.1, pred[]{:T(512)S(6)} %eq.11), kind=kOutput, calls=%fused_computation.11 | convolution fusion | flops 943652864 | bytes 5636105 | tf_op jit(solution)/shard_map/dot_general | solution.py:15
  21.3 5.3 %fusion.103 = (f32[1024]{0:T(1024)S(1)}, f32[1024]{0:T(1024)S(1)}, f32[256,1024]{1,0:T(8,128)S(1)}) fusion(f32[256,1024]{1,0:T(8,128)S(1)} %fusion.10, bf16[3584,2048]{1,0:T(8,128)(2,1)} %param.6, s32[]{:T(128)S(6)} %select_n.121, s32[]{:T(128)S(6)} %select_n.123, bf16[128,1792]{1,0:T(8,128)(2,1)S(1)} %collective-permute-done, ...), kind=kOutput, calls=%fused_computation.174 | convolution fusion | flops 944699392 | bytes 6692873 | tf_op jit(solution)/shard_map/dot_general | solution.py:15
  30.4 2.9 %collective-permute-start.4 = (f32[2,1024]{1,0:T(2,128)S(1)}, f32[2,1024]{1,0:T(2,128)S(1)}, u32[]{:S(2)}, u32[]{:S(2)}) collective-permute-start(f32[2,1024]{1,0:T(2,128)S(1)} %fusion.99), channel_id=1, source_target_pairs={{0,16},{8,24},{16,0},{24,8},{1,17},{9,25},{17,1},{25,9},{2,18},{10... | collective-permute-start | bytes 24584 | tf_op jit(solution)/shard_map/ppermute | solution.py:25
  43.3 2.4 %collective-permute-start.10 = (f32[2,1024]{1,0:T(2,128)S(1)}, f32[2,1024]{1,0:T(2,128)S(1)}, u32[]{:S(2)}, u32[]{:S(2)}) collective-permute-start(f32[2,1024]{1,0:T(2,128)S(1)} %fusion.98), channel_id=1, source_target_pairs={{0,16},{8,24},{16,0},{24,8},{1,17},{9,25},{17,1},{25,9},{2,18},{10... | collective-permute-start | bytes 24584 | tf_op jit(solution)/shard_map/ppermute | solution.py:25
  54.7 3.4 %collective-permute-start.12 = (bf16[256,1024]{1,0:T(8,128)(2,1)}, bf16[256,1024]{1,0:T(8,128)(2,1)}, u32[]{:S(2)}, u32[]{:S(2)}) collective-permute-start(bf16[256,1024]{1,0:T(8,128)(2,1)} %get-tuple-element.18), channel_id=1, source_target_pairs={{0,8},{8,0},{16,24},{24,16},{1,9},{9,1},{17,25},{25,17},{2,10},{10... | collective-permute-start | bytes 1572872 | tf_op jit(solution)/shard_map/ppermute | solution.py:25
  58.5 5.2 %collective-permute-done.23 = bf16[256,1024]{1,0:T(8,128)(2,1)} collective-permute-done((bf16[256,1024]{1,0:T(8,128)(2,1)S(1)}, bf16[256,1024]{1,0:T(8,128)(2,1)}, u32[]{:S(2)}, u32[]{:S(2)}) %collective-permute-start.23) | collective-permute-done | bytes 524320 | tf_op jit(solution)/shard_map/ppermute | solution.py:25
  72.3 2.7 %collective-permute-done.12 = bf16[256,1024]{1,0:T(8,128)(2,1)} collective-permute-done((bf16[256,1024]{1,0:T(8,128)(2,1)}, bf16[256,1024]{1,0:T(8,128)(2,1)}, u32[]{:S(2)}, u32[]{:S(2)}) %collective-permute-start.12) | collective-permute-done | bytes 524320 | tf_op jit(solution)/shard_map/ppermute | solution.py:25
  77.7 3.4 %collective-permute-start.29 = (bf16[128,1024]{1,0:T(8,128)(2,1)S(1)}, bf16[128,1024]{1,0:T(8,128)(2,1)S(1)}, u32[]{:S(2)}, u32[]{:S(2)}) collective-permute-start(bf16[128,1024]{1,0:T(8,128)(2,1)S(1)} %slice.39), channel_id=1, source_target_pairs={{0,8},{8,0},{16,24},{24,16},{1,9},{9,1},{17,25},{25,17},{2,10},{10... | collective-permute-start | bytes 786440 | tf_op jit(solution)/shard_map/ppermute | solution.py:25
  89.5 3.3 %collective-permute-start.18 = (bf16[128,1024]{1,0:T(8,128)(2,1)S(1)}, bf16[128,1024]{1,0:T(8,128)(2,1)S(1)}, u32[]{:S(2)}, u32[]{:S(2)}) collective-permute-start(bf16[128,1024]{1,0:T(8,128)(2,1)S(1)} %slice.37), channel_id=1, source_target_pairs={{0,8},{8,0},{16,24},{24,16},{1,9},{9,1},{17,25},{25,17},{2,10},{10... | collective-permute-start | bytes 786440 | tf_op jit(solution)/shard_map/ppermute | solution.py:25
  94.6 9.5 %collective-permute-done.14 = bf16[256,1024]{1,0:T(8,128)(2,1)S(1)} collective-permute-done((bf16[256,1024]{1,0:T(8,128)(2,1)}, bf16[256,1024]{1,0:T(8,128)(2,1)S(1)}, u32[]{:S(2)}, u32[]{:S(2)}) %collective-permute-start.14) | collective-permute-done | bytes 524320 | tf_op jit(solution)/shard_map/ppermute | solution.py:86
  109.8 10.5 %collective-permute-done.36 = bf16[256,1024]{1,0:T(8,128)(2,1)S(1)} collective-permute-done((bf16[256,1024]{1,0:T(8,128)(2,1)}, bf16[256,1024]{1,0:T(8,128)(2,1)S(1)}, u32[]{:S(2)}, u32[]{:S(2)}) %collective-permute-start.36) | collective-permute-done | bytes 524320 | tf_op jit(solution)/shard_map/ppermute | solution.py:88
  122.9 2.9 %collective-permute-done.31 = bf16[256,1024]{1,0:T(8,128)(2,1)S(1)} collective-permute-done((bf16[256,1024]{1,0:T(8,128)(2,1)S(1)}, bf16[256,1024]{1,0:T(8,128)(2,1)S(1)}, u32[]{:S(2)}, u32[]{:S(2)}) %collective-permute-start.31) | collective-permute-done | bytes 524320 | tf_op jit(solution)/shard_map/ppermute | solution.py:88
  129.5 3.4 %collective-permute-done.37 = bf16[256,1024]{1,0:T(8,128)(2,1)S(1)} collective-permute-done((bf16[256,1024]{1,0:T(8,128)(2,1)S(1)}, bf16[256,1024]{1,0:T(8,128)(2,1)S(1)}, u32[]{:S(2)}, u32[]{:S(2)}) %collective-permute-start.37) | collective-permute-done | bytes 524320 | tf_op jit(solution)/shard_map/ppermute | solution.py:20
  137.3 4.1 %collective-permute-done.48 = bf16[128,512]{1,0:T(8,128)(2,1)S(1)} collective-permute-done((bf16[128,512]{1,0:T(8,128)(2,1)S(1)}, bf16[128,512]{1,0:T(8,128)(2,1)S(1)}, u32[]{:S(2)}, u32[]{:S(2)}) %collective-permute-start.48) | collective-permute-done | bytes 131104 | tf_op jit(solution)/shard_map/ppermute | solution.py:20
  144.3 5.2 %collective-permute-done.45 = bf16[128,1536]{1,0:T(8,128)(2,1)S(1)} collective-permute-done((bf16[128,1536]{1,0:T(8,128)(2,1)S(1)}, bf16[128,1536]{1,0:T(8,128)(2,1)S(1)}, u32[]{:S(2)}, u32[]{:S(2)}) %collective-permute-start.45) | collective-permute-done | bytes 393248 | tf_op jit(solution)/shard_map/ppermute | solution.py:20
  154.4 2.4 %collective-permute-done.50 = f32[2,1024]{1,0:T(2,128)S(1)} collective-permute-done((f32[2,1024]{1,0:T(2,128)S(1)}, f32[2,1024]{1,0:T(2,128)S(1)}, u32[]{:S(2)}, u32[]{:S(2)}) %collective-permute-start.50) | collective-permute-done | bytes 8224 | tf_op jit(solution)/shard_map/ppermute | solution.py:25
  157.6 3.8 %collective-permute-done.51 = f32[2,1024]{1,0:T(2,128)S(1)} collective-permute-done((f32[2,1024]{1,0:T(2,128)S(1)}, f32[2,1024]{1,0:T(2,128)S(1)}, u32[]{:S(2)}, u32[]{:S(2)}) %collective-permute-start.51) | collective-permute-done | bytes 8224 | tf_op jit(solution)/shard_map/ppermute | solution.py:25
  167.9 2.8 %fusion.101 = (f32[1024]{0:T(1024)S(1)}, f32[1024]{0:T(1024)S(1)}, f32[256,1024]{1,0:T(8,128)S(1)}) fusion(f32[1024]{0:T(1024)S(1)} %bitcast.33, f32[256,1024]{1,0:T(8,128)S(1)} %copy-done.2, f32[1024]{0:T(1024)S(1)} %bitcast.30, f32[1024]{0:T(1024)S(1)} %convert_subtract_fusion, bf16[256,1024]{1,0:T(8,128)(2,1)} %get-tuple-element.18, ...), kind=kOutput, calls=%fused_computation.172 | convolution fusion | flops 811464704 | bytes 7622657 | tf_op jit(solution)/shard_map/dot_general | solution.py:15
  176.4 2.8 %collective-permute-done.39 = f32[2,1024]{1,0:T(2,128)S(1)} collective-permute-done((f32[2,1024]{1,0:T(2,128)S(1)}, f32[2,1024]{1,0:T(2,128)S(1)}, u32[]{:S(2)}, u32[]{:S(2)}) %collective-permute-start.39) | collective-permute-done | bytes 8224 | tf_op jit(solution)/shard_map/ppermute | solution.py:25
  191.8 2.4 %collective-permute-start.57 = (f32[1]{0:T(128)}, f32[1]{0:T(128)}, u32[]{:S(2)}, u32[]{:S(2)}) collective-permute-start(f32[1]{0:T(128)} %add.218), channel_id=1, source_target_pairs={{0,1},{1,0},{2,3},{3,2},{4,5},{5,4},{6,7},{7,6},{8,9},{9,8},{10,11... | collective-permute-start | bytes 20 | tf_op jit(solution)/shard_map/ppermute | solution.py:25
  198.6 11.3 %collective-permute-done.55 = bf16[128,1792]{1,0:T(8,128)(2,1)S(1)} collective-permute-done((bf16[128,1792]{1,0:T(8,128)(2,1)S(1)}, bf16[128,1792]{1,0:T(8,128)(2,1)S(1)}, u32[]{:S(2)}, u32[]{:S(2)}) %collective-permute-start.55) | collective-permute-done | bytes 458784 | tf_op jit(solution)/shard_map/ppermute | solution.py:20
  210.9 6.8 %collective-permute-done.43 = bf16[128,1792]{1,0:T(8,128)(2,1)S(1)} collective-permute-done((bf16[128,1792]{1,0:T(8,128)(2,1)S(1)}, bf16[128,1792]{1,0:T(8,128)(2,1)S(1)}, u32[]{:S(2)}, u32[]{:S(2)}) %collective-permute-start.43) | collective-permute-done | bytes 458784 | tf_op jit(solution)/shard_map/ppermute | solution.py:20
  (216 shorter events, 100.6 us)
Async XLA Ops:
  14.9 18.4 %collective-permute-start.6 = (bf16[128,1792]{1,0:T(8,128)(2,1)}, bf16[128,1792]{1,0:T(8,128)(2,1)S(1)}, u32[]{:S(2)}, u32[]{:S(2)}) collective-permute-start(bf16[128,1792]{1,0:T(8,128)(2,1)} %param.5), channel_id=1, source_target_pairs={{0,2},{2,0},{1,3},{3,1},{4,6},{6,4},{5,7},{7,5},{8,10},{10,8},{9,1... | collective-permute-start | bytes 1376264 | tf_op jit(solution)/shard_map/ppermute | solution.py:25
  48.7 15.0 %collective-permute-start.23 = (bf16[256,1024]{1,0:T(8,128)(2,1)S(1)}, bf16[256,1024]{1,0:T(8,128)(2,1)}, u32[]{:S(2)}, u32[]{:S(2)}) collective-permute-start(bf16[256,1024]{1,0:T(8,128)(2,1)S(1)} %get-tuple-element.22), channel_id=1, source_target_pairs={{0,8},{8,0},{16,24},{24,16},{1,9},{9,1},{17,25},{25,17},{2,10},{10... | collective-permute-start | bytes 1572872 | tf_op jit(solution)/shard_map/ppermute | solution.py:25
  50.5 14.7 %collective-permute-start.24 = (bf16[256,1024]{1,0:T(8,128)(2,1)S(1)}, bf16[256,1024]{1,0:T(8,128)(2,1)}, u32[]{:S(2)}, u32[]{:S(2)}) collective-permute-start(bf16[256,1024]{1,0:T(8,128)(2,1)S(1)} %get-tuple-element.22), channel_id=1, source_target_pairs={{8,16},{16,8},{9,17},{17,9},{10,18},{18,10},{11,19},{19,11},{12,20... | collective-permute-start | bytes 1572872 | tf_op jit(solution)/shard_map/ppermute | solution.py:84
  51.9 14.9 %collective-permute-start.27 = (bf16[256,1024]{1,0:T(8,128)(2,1)S(1)}, bf16[256,1024]{1,0:T(8,128)(2,1)S(1)}, u32[]{:S(2)}, u32[]{:S(2)}) collective-permute-start(bf16[256,1024]{1,0:T(8,128)(2,1)S(1)} %get-tuple-element.22), channel_id=1, source_target_pairs={{0,4},{4,0},{1,5},{5,1},{2,6},{6,2},{3,7},{7,3},{8,12},{12,8},{9,1... | collective-permute-start | bytes 1572872 | tf_op jit(solution)/shard_map/ppermute | solution.py:20
  54.7 20.3 %collective-permute-start.12 = (bf16[256,1024]{1,0:T(8,128)(2,1)}, bf16[256,1024]{1,0:T(8,128)(2,1)}, u32[]{:S(2)}, u32[]{:S(2)}) collective-permute-start(bf16[256,1024]{1,0:T(8,128)(2,1)} %get-tuple-element.18), channel_id=1, source_target_pairs={{0,8},{8,0},{16,24},{24,16},{1,9},{9,1},{17,25},{25,17},{2,10},{10... | collective-permute-start | bytes 1572872 | tf_op jit(solution)/shard_map/ppermute | solution.py:25
  58.0 19.6 %collective-permute-start.16 = (bf16[256,1024]{1,0:T(8,128)(2,1)}, bf16[256,1024]{1,0:T(8,128)(2,1)}, u32[]{:S(2)}, u32[]{:S(2)}) collective-permute-start(bf16[256,1024]{1,0:T(8,128)(2,1)} %get-tuple-element.18), channel_id=1, source_target_pairs={{0,4},{4,0},{1,5},{5,1},{2,6},{6,2},{3,7},{7,3},{8,12},{12,8},{9,1... | collective-permute-start | bytes 1572872 | tf_op jit(solution)/shard_map/ppermute | solution.py:20
  63.8 19.3 %collective-permute-start.13 = (bf16[256,1024]{1,0:T(8,128)(2,1)}, bf16[256,1024]{1,0:T(8,128)(2,1)}, u32[]{:S(2)}, u32[]{:S(2)}) collective-permute-start(bf16[256,1024]{1,0:T(8,128)(2,1)} %get-tuple-element.18), channel_id=1, source_target_pairs={{8,16},{16,8},{9,17},{17,9},{10,18},{18,10},{11,19},{19,11},{12,20... | collective-permute-start | bytes 1572872 | tf_op jit(solution)/shard_map/ppermute | solution.py:84
  65.2 21.0 %collective-permute-start.25 = (bf16[256,1024]{1,0:T(8,128)(2,1)}, bf16[256,1024]{1,0:T(8,128)(2,1)}, u32[]{:S(2)}, u32[]{:S(2)}) collective-permute-start(bf16[256,1024]{1,0:T(8,128)(2,1)} %collective-permute-done.24), channel_id=1, source_target_pairs={{8,0},{16,24},{9,1},{17,25},{10,2},{18,26},{11,3},{19,27},{12,4},{... | collective-permute-start | bytes 1572872 | tf_op jit(solution)/shard_map/ppermute | solution.py:86
  67.6 19.3 %collective-permute-start.26 = (bf16[256,1024]{1,0:T(8,128)(2,1)}, bf16[256,1024]{1,0:T(8,128)(2,1)}, u32[]{:S(2)}, u32[]{:S(2)}) collective-permute-start(bf16[256,1024]{1,0:T(8,128)(2,1)} %collective-permute-done.23), channel_id=1, source_target_pairs={{8,16},{16,8},{9,17},{17,9},{10,18},{18,10},{11,19},{19,11},{12,20... | collective-permute-start | bytes 1572872 | tf_op jit(solution)/shard_map/ppermute | solution.py:85
  77.7 15.2 %collective-permute-start.29 = (bf16[128,1024]{1,0:T(8,128)(2,1)S(1)}, bf16[128,1024]{1,0:T(8,128)(2,1)S(1)}, u32[]{:S(2)}, u32[]{:S(2)}) collective-permute-start(bf16[128,1024]{1,0:T(8,128)(2,1)S(1)} %slice.39), channel_id=1, source_target_pairs={{0,8},{8,0},{16,24},{24,16},{1,9},{9,1},{17,25},{25,17},{2,10},{10... | collective-permute-start | bytes 786440 | tf_op jit(solution)/shard_map/ppermute | solution.py:25
  83.1 25.0 %collective-permute-start.17 = (bf16[128,1024]{1,0:T(8,128)(2,1)S(1)}, bf16[128,1024]{1,0:T(8,128)(2,1)S(1)}, u32[]{:S(2)}, u32[]{:S(2)}) collective-permute-start(bf16[128,1024]{1,0:T(8,128)(2,1)S(1)} %slice.36), channel_id=1, source_target_pairs={{0,4},{4,0},{1,5},{5,1},{2,6},{6,2},{3,7},{7,3},{8,12},{12,8},{9,1... | collective-permute-start | bytes 786440 | tf_op jit(solution)/shard_map/ppermute | solution.py:20
  86.2 19.2 %collective-permute-start.15 = (bf16[256,1024]{1,0:T(8,128)(2,1)}, bf16[256,1024]{1,0:T(8,128)(2,1)S(1)}, u32[]{:S(2)}, u32[]{:S(2)}) collective-permute-start(bf16[256,1024]{1,0:T(8,128)(2,1)} %collective-permute-done.12), channel_id=1, source_target_pairs={{8,16},{16,8},{9,17},{17,9},{10,18},{18,10},{11,19},{19,11},{12,20... | collective-permute-start | bytes 1572872 | tf_op jit(solution)/shard_map/ppermute | solution.py:85
  86.9 17.2 %collective-permute-start.14 = (bf16[256,1024]{1,0:T(8,128)(2,1)}, bf16[256,1024]{1,0:T(8,128)(2,1)S(1)}, u32[]{:S(2)}, u32[]{:S(2)}) collective-permute-start(bf16[256,1024]{1,0:T(8,128)(2,1)} %collective-permute-done.13), channel_id=1, source_target_pairs={{8,0},{16,24},{9,1},{17,25},{10,2},{18,26},{11,3},{19,27},{12,4},{... | collective-permute-start | bytes 1572872 | tf_op jit(solution)/shard_map/ppermute | solution.py:86
  89.5 20.3 %collective-permute-start.18 = (bf16[128,1024]{1,0:T(8,128)(2,1)S(1)}, bf16[128,1024]{1,0:T(8,128)(2,1)S(1)}, u32[]{:S(2)}, u32[]{:S(2)}) collective-permute-start(bf16[128,1024]{1,0:T(8,128)(2,1)S(1)} %slice.37), channel_id=1, source_target_pairs={{0,8},{8,0},{16,24},{24,16},{1,9},{9,1},{17,25},{25,17},{2,10},{10... | collective-permute-start | bytes 786440 | tf_op jit(solution)/shard_map/ppermute | solution.py:25
  92.8 28.8 %collective-permute-start.30 = (bf16[256,1024]{1,0:T(8,128)(2,1)S(1)}, bf16[256,1024]{1,0:T(8,128)(2,1)S(1)}, u32[]{:S(2)}, u32[]{:S(2)}) collective-permute-start(bf16[256,1024]{1,0:T(8,128)(2,1)S(1)} %get-tuple-element.20), channel_id=1, source_target_pairs={{0,4},{4,0},{1,5},{5,1},{2,6},{6,2},{3,7},{7,3},{8,12},{12,8},{9,1... | collective-permute-start | bytes 1572872 | tf_op jit(solution)/shard_map/ppermute | solution.py:20
  104.1 16.1 %collective-permute-start.36 = (bf16[256,1024]{1,0:T(8,128)(2,1)}, bf16[256,1024]{1,0:T(8,128)(2,1)S(1)}, u32[]{:S(2)}, u32[]{:S(2)}) collective-permute-start(bf16[256,1024]{1,0:T(8,128)(2,1)} %collective-permute-done.26), channel_id=1, source_target_pairs={{8,0},{16,24},{9,1},{17,25},{10,2},{18,26},{11,3},{19,27},{12,4},{... | collective-permute-start | bytes 1572872 | tf_op jit(solution)/shard_map/ppermute | solution.py:88
  105.6 21.6 %collective-permute-start.19 = (bf16[256,1024]{1,0:T(8,128)(2,1)S(1)}, bf16[256,1024]{1,0:T(8,128)(2,1)S(1)}, u32[]{:S(2)}, u32[]{:S(2)}) collective-permute-start(bf16[256,1024]{1,0:T(8,128)(2,1)S(1)} %get-tuple-element.16), channel_id=1, source_target_pairs={{0,4},{4,0},{1,5},{5,1},{2,6},{6,2},{3,7},{7,3},{8,12},{12,8},{9,1... | collective-permute-start | bytes 1572872 | tf_op jit(solution)/shard_map/ppermute | solution.py:20
  108.1 17.7 %collective-permute-start.31 = (bf16[256,1024]{1,0:T(8,128)(2,1)S(1)}, bf16[256,1024]{1,0:T(8,128)(2,1)S(1)}, u32[]{:S(2)}, u32[]{:S(2)}) collective-permute-start(bf16[256,1024]{1,0:T(8,128)(2,1)S(1)} %collective-permute-done.15), channel_id=1, source_target_pairs={{8,0},{16,24},{9,1},{17,25},{10,2},{18,26},{11,3},{19,27},{12,4},{... | collective-permute-start | bytes 1572872 | tf_op jit(solution)/shard_map/ppermute | solution.py:88
  125.9 15.7 %collective-permute-start.32 = (bf16[256,1024]{1,0:T(8,128)(2,1)S(1)}, bf16[256,1024]{1,0:T(8,128)(2,1)S(1)}, u32[]{:S(2)}, u32[]{:S(2)}) collective-permute-start(bf16[256,1024]{1,0:T(8,128)(2,1)S(1)} %broadcast_select_fusion.1), channel_id=1, source_target_pairs={{0,4},{4,0},{1,5},{5,1},{2,6},{6,2},{3,7},{7,3},{8,12},{12,8},{9,1... | collective-permute-start | bytes 1572872 | tf_op jit(solution)/shard_map/ppermute | solution.py:20
  129.4 23.7 %collective-permute-start.20 = (f32[128,1536]{1,0:T(8,128)S(1)}, f32[128,1536]{1,0:T(8,128)S(1)}, u32[]{:S(2)}, u32[]{:S(2)}) collective-permute-start(f32[128,1536]{1,0:T(8,128)S(1)} %constant_dynamic-slice_fusion.7), channel_id=1, source_target_pairs={{0,2},{2,0},{1,3},{3,1},{4,6},{6,4},{5,7},{7,5},{8,10},{10,8},{9,1... | collective-permute-start | bytes 2359304 | tf_op jit(solution)/shard_map/ppermute | solution.py:25
  176.3 19.9 %collective-permute-start.54 = (f32[128,1792]{1,0:T(8,128)S(1)}, f32[128,1792]{1,0:T(8,128)S(1)}, u32[]{:S(2)}, u32[]{:S(2)}) collective-permute-start(f32[128,1792]{1,0:T(8,128)S(1)} %constant_dynamic-slice_fusion), channel_id=1, source_target_pairs={{0,2},{2,0},{1,3},{3,1},{4,6},{6,4},{5,7},{7,5},{8,10},{10,8},{9,1... | collective-permute-start | bytes 2752520 | tf_op jit(solution)/shard_map/ppermute | solution.py:25
  181.1 17.5 %collective-permute-start.53 = (f32[128,1792]{1,0:T(8,128)S(1)}, f32[128,1792]{1,0:T(8,128)S(1)}, u32[]{:S(2)}, u32[]{:S(2)}) collective-permute-start(f32[128,1792]{1,0:T(8,128)S(1)} %constant_dynamic-slice_fusion.1), channel_id=1, source_target_pairs={{0,2},{2,0},{1,3},{3,1},{4,6},{6,4},{5,7},{7,5},{8,10},{10,8},{9,1... | collective-permute-start | bytes 2752520 | tf_op jit(solution)/shard_map/ppermute | solution.py:25
  187.6 23.3 %collective-permute-start.41 = (f32[128,1792]{1,0:T(8,128)S(1)}, f32[128,1792]{1,0:T(8,128)S(1)}, u32[]{:S(2)}, u32[]{:S(2)}) collective-permute-start(f32[128,1792]{1,0:T(8,128)S(1)} %constant_dynamic-slice_fusion.5), channel_id=1, source_target_pairs={{0,2},{2,0},{1,3},{3,1},{4,6},{6,4},{5,7},{7,5},{8,10},{10,8},{9,1... | collective-permute-start | bytes 2752520 | tf_op jit(solution)/shard_map/ppermute | solution.py:25
  197.6 20.1 %collective-permute-start.43 = (bf16[128,1792]{1,0:T(8,128)(2,1)S(1)}, bf16[128,1792]{1,0:T(8,128)(2,1)S(1)}, u32[]{:S(2)}, u32[]{:S(2)}) collective-permute-start(bf16[128,1792]{1,0:T(8,128)(2,1)S(1)} %add_convert_fusion.1), channel_id=1, source_target_pairs={{0,1},{1,0},{2,3},{3,2},{4,5},{5,4},{6,7},{7,6},{8,9},{9,8},{10,11... | collective-permute-start | bytes 1376264 | tf_op jit(solution)/shard_map/ppermute | solution.py:20
  (54 other events, 505.8 us)
where the time goes:
time: 221 us; the launch traced here: 220 us
  waiting for transfers between devices  97.1 us (44%)
  starting transfers between devices  67.1 us (30%)
  matrix products  33 us (15%)
  other arithmetic  9.24 us (4%)
  local copies, waits for them, and re-layouts  8.84 us (4%)
  between operations  4.63 us (2%)
    ppermute x16, waiting for transfers between devices, shift(): return lax.ppermute(x, axis, [(i, (i + step) % size) for i in range(size)])  41.8 us
    ppermute x34, starting transfers between devices, flip(): return lax.ppermute(x, axis, [(i, i ^ bit) for i in range(size)])  34.7 us
    dot_general x16, matrix products, dot(): return lax.dot_general(a, b, (dims, ((), ())), preferred_element_type=F32)  33 us
    ppermute x34, waiting for transfers between devices, flip(): return lax.ppermute(x, axis, [(i, i ^ bit) for i in range(size)])  30 us
    ppermute x16, starting transfers between devices, shift(): return lax.ppermute(x, axis, [(i, (i + step) % size) for i in range(size)])  22 us
    ppermute x2, waiting for transfers between devices, gather_rows(): last_end = lax.ppermute(far_in, 'z', [(1, 0), (2, 3)])  13.4 us
    ppermute x2, waiting for transfers between devices, gather_rows(): far_end = lax.ppermute(mid, 'z', [(1, 0), (2, 3)])  11.9 us
  transfers between devices with their start and end apart: 58, of which 26 were waited for; matrix products, arithmetic and copies ran while one was open for 21% of the time, Pallas kernels for 0%

commit v1 on v0

--- a/solution.py
+++ b/solution.py
@@ -34,6 +34,10 @@
     return x
 
 
+def hold(x, *first):
+    return lax.optimization_barrier((x, *first))[0]
+
+
 def own_block(x, index, count, axis):
     size = x.shape[axis] // count
     return lax.dynamic_slice_in_dim(x, index * size, size, axis)
@@ -61,8 +65,7 @@
     return [shift(x, "feat", step) for step in range(1, lax.axis_size("feat"))]
 
 
-def project(mine, others, weights):
-    z = dot(both_cores(mine), weights[0], ((1,), (0,)))
+def project(z, others, weights):
     for other, weight in zip(others, weights[1:]):
         z = z + dot(both_cores(other), weight, ((1,), (0,)))
     return z
@@ -87,13 +90,13 @@
     far = jnp.where(end, far_end, far_in)
     last_end = lax.ppermute(far_in, "z", [(1, 0), (2, 3)])
     last = jnp.where(end, last_end, mid)
-    early, late = [own, near, far], [last]
+    first, second, third = [own, near], [far], [last]
     for step in range(1, lax.axis_size("y")):
         y_own = shift(own, "y", step)
-        y_near = [shift(near[:half], "y", step), flip(y_own[half:], "z")]
-        early += [y_own, *y_near, shift(far, "y", step)]
-        late += [shift(last, "y", step)]
-    return jnp.concatenate(early, 0), jnp.concatenate(late, 0)
+        first += [y_own, shift(near[:half], "y", step), flip(y_own[half:], "z")]
+        second += [shift(far, "y", step)]
+        third += [shift(last, "y", step)]
+    return [jnp.concatenate(blocks, 0) for blocks in (first, second, third)]
 
 
 def gram_rows(half, rows):
@@ -110,16 +113,21 @@
     return (inverse * (d - mean - normed * tilt)).astype(BF16), tilt
 
 
-def embed_grad(back, weights):
+def embed_parts(back, weights):
+    return [add_cores(dot(back, weight, ((1,), (1,)))).astype(BF16) for weight in weights[1:]]
+
+
+def swap_parts(sent):
     num_feat = lax.axis_size("feat")
-    others = []
-    for step in range(1, num_feat):
-        part = add_cores(dot(back, weights[step], ((1,), (1,))))
-        others.append(shift(part.astype(BF16), "feat", num_feat - step))
-    grad = add_cores(dot(back, weights[0], ((1,), (1,))))
-    for other in others:
-        grad = grad + other.astype(F32)
-    return grad
+    return [
+        [shift(piece, "feat", num_feat - step) for step, piece in enumerate(pieces, 1)]
+        for pieces in zip(*[jnp.split(part, [part.shape[0] * 3 // 4]) for part in sent])
+    ]
+
+
+def embed_grad(own, got):
+    pieces = jnp.split(own, [own.shape[0] * 3 // 4])
+    return jnp.concatenate([piece + sum(part.astype(F32) for part in parts) for piece, parts in zip(pieces, got)], 0)
 
 
 def body(table, text, table_proj, text_proj):
@@ -129,13 +137,15 @@
     text_weights = weight_blocks(text_proj)
 
     others_table = swap_feat(table)
-    text, others_table = lax.optimization_barrier((text, others_table))
+    z_table = dot(both_cores(table), table_weights[0], ((1,), (0,)))
+    z_text = dot(both_cores(text), text_weights[0], ((1,), (0,)))
+    text, z_table, z_text, *others_table = lax.optimization_barrier((text, z_table, z_text, *others_table))
     others_text = swap_feat(text)
 
-    normed_table, inverse_table = normalize(project(table, others_table, table_weights), pairs)
+    normed_table, inverse_table = normalize(project(z_table, others_table, table_weights), pairs)
     half_table = normed_table.astype(BF16)
     all_table = gather_rows(half_table)
-    normed_text, inverse_text = normalize(project(text, others_text, text_weights), pairs)
+    normed_text, inverse_text = normalize(project(z_text, others_text, text_weights), pairs)
     half_text = normed_text.astype(BF16)
     all_text = gather_rows(half_text)
 
@@ -153,18 +163,27 @@
         off_text = off_text + dot(gram, rows, ((1,), (0,)))
     d_text = (OFF_WEIGHT / pairs) * off_text + half_table.astype(F32) * diag_weight
     back_text, _ = backward(d_text, normed_text, inverse_text, pairs)
-    grad_text = embed_grad(back_text, text_weights)
+    sent_text = embed_parts(back_text, text_weights)
+    got_text = swap_parts(sent_text)
 
     off_table = 0.0
     for gram, rows in zip(gram_text, all_table):
         off_table = off_table + dot(gram, rows, ((1,), (0,)))
     d_table = (OFF_WEIGHT / pairs) * off_table + half_text.astype(F32) * diag_weight
+    d_table = hold(d_table, *sent_text)
     back_table, tilt_table = backward(d_table, normed_table, inverse_table, pairs)
-    grad_table = embed_grad(back_table, table_weights)
+    own_text = add_cores(dot(hold(back_text, *sent_text), text_weights[0], ((1,), (1,))))
+    back_table, *got_text[0] = lax.optimization_barrier((back_table, *got_text[0]))
+    sent_table = embed_parts(back_table, table_weights)
+    *sent_table, got_text[1] = lax.optimization_barrier((*sent_table, got_text[1]))
+    got_table = swap_parts(sent_table)
+    own_table = add_cores(dot(hold(back_table, *sent_table), table_weights[0], ((1,), (1,))))
+    grad_text = embed_grad(own_text, got_text)
+    grad_table = embed_grad(own_table, got_table)
 
     squares = tilt_table - diag_weight * diag
     terms = (1.0 - diag) * (1.0 - diag) - OFF_WEIGHT * diag * diag + squares
-    loss_total = cube_sum(jnp.sum(terms).reshape(1), "core", "feat")
+    loss_total = cube_sum(hold(jnp.sum(terms).reshape(1), *sent_table), "core", "feat")
     return grad_table, grad_text, loss_total / features
 
 

time: 221 us -> 234 us (1.059)
  matrix products: 33 us -> 40.4 us
  waiting for transfers between devices: 97.1 us -> 102 us
  starting transfers between devices: 67.1 us -> 71.2 us
  local copies, waits for them, and re-layouts: 8.84 us -> 5.6 us
    ppermute x34 -> x38, waiting for transfers between devices: 30 us -> 42.7 us  [flip(): return lax.ppermute(x, axis, [(i, i ^ bit) for i in range(size)])]
    ppermute x2, waiting for transfers between devices: 13.4 us -> 1.75 us  [gather_rows(): last_end = lax.ppermute(far_in, 'z', [(1, 0), (2, 3)])]
    dot_general x16 -> x20, matrix products: 33 us -> 40.4 us  [dot(): return lax.dot_general(a, b, (dims, ((), ())), preferred_element_type=F32)]
    ppermute x2, waiting for transfers between devices: 11.9 us -> 19.1 us  [gather_rows(): far_end = lax.ppermute(mid, 'z', [(1, 0), (2, 3)])]
    ppermute x34 -> x38, starting transfers between devices: 34.7 us -> 39.6 us  [flip(): return lax.ppermute(x, axis, [(i, i ^ bit) for i in range(size)])]
    ppermute x16 -> x20, waiting for transfers between devices: 41.8 us -> 38.1 us  [shift(): return lax.ppermute(x, axis, [(i, (i + step) % size) for i in range(size)])]
    ppermute x16 -> x20, starting transfers between devices: 22 us -> 23.5 us  [shift(): return lax.ppermute(x, axis, [(i, (i + step) % size) for i in range(size)])]
  transfers between devices with their start and end apart: 58 -> 66, of which waited for: 26 -> 33; matrix products, arithmetic and copies ran while one was open for 21% -> 20% of each run, Pallas kernels for 0% -> 0%
where the time goes in v1:
time: 234 us; the launch traced here: 233 us
  waiting for transfers between devices  102 us (44%)
  starting transfers between devices  71.2 us (30%)
  matrix products  40.4 us (17%)
  other arithmetic  9.65 us (4%)
  local copies, waits for them, and re-layouts  5.6 us (2%)
  between operations  4.79 us (2%)
    ppermute x38, waiting for transfers between devices, flip(): return lax.ppermute(x, axis, [(i, i ^ bit) for i in range(size)])  42.7 us
    dot_general x20, matrix products, dot(): return lax.dot_general(a, b, (dims, ((), ())), preferred_element_type=F32)  40.4 us
    ppermute x38, starting transfers between devices, flip(): return lax.ppermute(x, axis, [(i, i ^ bit) for i in range(size)])  39.6 us
    ppermute x20, waiting for transfers between devices, shift(): return lax.ppermute(x, axis, [(i, (i + step) % size) for i in range(size)])  38.1 us
    ppermute x20, starting transfers between devices, shift(): return lax.ppermute(x, axis, [(i, (i + step) % size) for i in range(size)])  23.5 us
    ppermute x2, waiting for transfers between devices, gather_rows(): far_end = lax.ppermute(mid, 'z', [(1, 0), (2, 3)])  19.1 us
  transfers between devices with their start and end apart: 66, of which 33 were waited for; matrix products, arithmetic and copies ran while one was open for 20% of the time, Pallas kernels for 0%

profile of v1, /device:TPU:0, one launch (start us, length us, event | category | flops | bytes accessed | tf_op | source)
XLA Modules:
  0.0 233.3 jit_solution(12577885315380588419)
XLA Ops:
  1.2 2.9 %collective-permute-start.2 = (bf16[128,1792]{1,0:T(8,128)(2,1)}, bf16[128,1792]{1,0:T(8,128)(2,1)S(1)}, u32[]{:S(2)}, u32[]{:S(2)}) collective-permute-start(bf16[128,1792]{1,0:T(8,128)(2,1)} %param.4), channel_id=1, source_target_pairs={{0,1},{1,0},{2,3},{3,2},{4,5},{5,4},{6,7},{7,6},{8,9},{9,8},{10,11... | collective-permute-start | bytes 1376264 | tf_op jit(solution)/shard_map/ppermute | solution.py:20
  4.1 5.7 %fusion.10 = f32[256,1024]{1,0:T(8,128)} fusion(bf16[3584,2048]{1,0:T(8,128)(2,1)} %param.7, s32[]{:T(128)S(6)} %select_n.131, s32[]{:T(128)S(6)} %select_n.133, bf16[128,1792]{1,0:T(8,128)(2,1)S(1)} %collective-permute-done.1, bf16[128,1792]{1,0:T(8,128)(2,1)} %param.5, pred[]{:T(512)S(6)} %eq.11), kind=kOutput, calls=%fused_computation.11 | convolution fusion | flops 943652864 | bytes 5636105 | tf_op jit(solution)/shard_map/dot_general | solution.py:15
  9.8 4.3 %fusion.14 = f32[256,1024]{1,0:T(8,128)S(1)} fusion(bf16[3584,2048]{1,0:T(8,128)(2,1)} %param.6, s32[]{:T(128)S(6)} %select_n.131, s32[]{:T(128)S(6)} %select_n.133, bf16[128,1792]{1,0:T(8,128)(2,1)S(1)} %collective-permute-done, bf16[128,1792]{1,0:T(8,128)(2,1)S(1)} %copy-done.1, pred[]{:T(512)S(6)} %eq.11), kind=kOutput, calls=%fused_computation.15 | convolution fusion | flops 943652864 | bytes 5636105 | tf_op jit(solution)/shard_map/dot_general | solution.py:15
  16.9 4.3 %fusion.6 = f32[256,1024]{1,0:T(8,128)S(1)} fusion(bf16[3584,2048]{1,0:T(8,128)(2,1)} %param.6, s32[]{:T(128)S(6)} %select_n.138, s32[]{:T(128)S(6)} %select_n.133, bf16[128,1792]{1,0:T(8,128)(2,1)S(1)} %collective-permute-done.3, bf16[128,1792]{1,0:T(8,128)(2,1)S(1)} %collective-permute-done.2, pred[]{:T(512)S(6)} %eq.11), kind=kOutput, calls=%fused_computation.7 | convolution fusion | flops 943652864 | bytes 5636105 | tf_op jit(solution)/shard_map/dot_general | solution.py:15
  25.2 2.9 %collective-permute-start.5 = (f32[2,1024]{1,0:T(2,128)S(1)}, f32[2,1024]{1,0:T(2,128)S(1)}, u32[]{:S(2)}, u32[]{:S(2)}) collective-permute-start(f32[2,1024]{1,0:T(2,128)S(1)} %fusion.120), channel_id=1, source_target_pairs={{0,16},{8,24},{16,0},{24,8},{1,17},{9,25},{17,1},{25,9},{2,18},{10... | collective-permute-start | bytes 24584 | tf_op jit(solution)/shard_map/ppermute | solution.py:25
  33.6 5.5 %fusion.123 = (f32[1024]{0:T(1024)S(1)}, f32[1024]{0:T(1024)S(1)}, f32[256,1024]{1,0:T(8,128)}) fusion(f32[256,1024]{1,0:T(8,128)S(1)} %copy-done.2, bf16[3584,2048]{1,0:T(8,128)(2,1)} %param.7, s32[]{:T(128)S(6)} %select_n.138, s32[]{:T(128)S(6)} %select_n.133, bf16[128,1792]{1,0:T(8,128)(2,1)S(1)} %collective-permute-done.8, ...), kind=kOutput, calls=%fused_computation.210 | convolution fusion | flops 944699392 | bytes 6692873 | tf_op jit(solution)/shard_map/dot_general | solution.py:15
  42.9 3.0 %collective-permute-start.10 = (f32[2,1024]{1,0:T(2,128)S(1)}, f32[2,1024]{1,0:T(2,128)S(1)}, u32[]{:S(2)}, u32[]{:S(2)}) collective-permute-start(f32[2,1024]{1,0:T(2,128)S(1)} %fusion.119), channel_id=1, source_target_pairs={{0,16},{8,24},{16,0},{24,8},{1,17},{9,25},{17,1},{25,9},{2,18},{10... | collective-permute-start | bytes 24584 | tf_op jit(solution)/shard_map/ppermute | solution.py:25
  47.4 4.1 %collective-permute-done.10 = f32[2,1024]{1,0:T(2,128)S(1)} collective-permute-done((f32[2,1024]{1,0:T(2,128)S(1)}, f32[2,1024]{1,0:T(2,128)S(1)}, u32[]{:S(2)}, u32[]{:S(2)}) %collective-permute-start.10) | collective-permute-done | bytes 8224 | tf_op jit(solution)/shard_map/ppermute | solution.py:25
  54.0 3.2 %collective-permute-done.11 = f32[2,1024]{1,0:T(2,128)S(1)} collective-permute-done((f32[2,1024]{1,0:T(2,128)S(1)}, f32[2,1024]{1,0:T(2,128)S(1)}, u32[]{:S(2)}, u32[]{:S(2)}) %collective-permute-start.11) | collective-permute-done | bytes 8224 | tf_op jit(solution)/shard_map/ppermute | solution.py:25
  63.4 6.0 %collective-permute-start.22 = (bf16[128,1024]{1,0:T(8,128)(2,1)S(1)}, bf16[128,1024]{1,0:T(8,128)(2,1)S(1)}, u32[]{:S(2)}, u32[]{:S(2)}) collective-permute-start(bf16[128,1024]{1,0:T(8,128)(2,1)S(1)} %slice.39), channel_id=1, source_target_pairs={{0,8},{8,0},{16,24},{24,16},{1,9},{9,1},{17,25},{25,17},{2,10},{10... | collective-permute-start | bytes 786440 | tf_op jit(solution)/shard_map/ppermute | solution.py:25
  72.3 4.2 %collective-permute-done.22 = bf16[128,1024]{1,0:T(8,128)(2,1)S(1)} collective-permute-done((bf16[128,1024]{1,0:T(8,128)(2,1)S(1)}, bf16[128,1024]{1,0:T(8,128)(2,1)S(1)}, u32[]{:S(2)}, u32[]{:S(2)}) %collective-permute-start.22) | collective-permute-done | bytes 262176 | tf_op jit(solution)/shard_map/ppermute | solution.py:25
  80.0 7.8 %collective-permute-done.12 = bf16[256,1024]{1,0:T(8,128)(2,1)S(1)} collective-permute-done((bf16[256,1024]{1,0:T(8,128)(2,1)S(1)}, bf16[256,1024]{1,0:T(8,128)(2,1)S(1)}, u32[]{:S(2)}, u32[]{:S(2)}) %collective-permute-start.12) | collective-permute-done | bytes 524320 | tf_op jit(solution)/shard_map/ppermute | solution.py:25
  88.5 10.5 %collective-permute-done.31 = bf16[256,1024]{1,0:T(8,128)(2,1)S(1)} collective-permute-done((bf16[256,1024]{1,0:T(8,128)(2,1)S(1)}, bf16[256,1024]{1,0:T(8,128)(2,1)S(1)}, u32[]{:S(2)}, u32[]{:S(2)}) %collective-permute-start.31) | collective-permute-done | bytes 524320 | tf_op jit(solution)/shard_map/ppermute | solution.py:89
  101.7 2.9 %collective-permute-done.15 = bf16[128,1024]{1,0:T(8,128)(2,1)S(1)} collective-permute-done((bf16[128,1024]{1,0:T(8,128)(2,1)S(1)}, bf16[128,1024]{1,0:T(8,128)(2,1)S(1)}, u32[]{:S(2)}, u32[]{:S(2)}) %collective-permute-start.15) | collective-permute-done | bytes 262176 | tf_op jit(solution)/shard_map/ppermute | solution.py:25
  108.0 8.5 %collective-permute-done.24 = bf16[256,1024]{1,0:T(8,128)(2,1)S(1)} collective-permute-done((bf16[256,1024]{1,0:T(8,128)(2,1)S(1)}, bf16[256,1024]{1,0:T(8,128)(2,1)S(1)}, u32[]{:S(2)}, u32[]{:S(2)}) %collective-permute-start.24) | collective-permute-done | bytes 524320 | tf_op jit(solution)/shard_map/ppermute | solution.py:89
  129.3 6.3 %collective-permute-done.45 = bf16[128,512]{1,0:T(8,128)(2,1)S(1)} collective-permute-done((bf16[128,512]{1,0:T(8,128)(2,1)S(1)}, bf16[128,512]{1,0:T(8,128)(2,1)S(1)}, u32[]{:S(2)}, u32[]{:S(2)}) %collective-permute-start.45) | collective-permute-done | bytes 131104 | tf_op jit(solution)/shard_map/ppermute | solution.py:20
  137.9 10.8 %collective-permute-done.40 = bf16[256,1024]{1,0:T(8,128)(2,1)S(1)} collective-permute-done((bf16[256,1024]{1,0:T(8,128)(2,1)S(1)}, bf16[256,1024]{1,0:T(8,128)(2,1)S(1)}, u32[]{:S(2)}, u32[]{:S(2)}) %collective-permute-start.40) | collective-permute-done | bytes 524320 | tf_op jit(solution)/shard_map/ppermute | solution.py:20
  154.6 3.5 %collective-permute-done.48 = bf16[128,512]{1,0:T(8,128)(2,1)S(1)} collective-permute-done((bf16[128,512]{1,0:T(8,128)(2,1)S(1)}, bf16[128,512]{1,0:T(8,128)(2,1)S(1)}, u32[]{:S(2)}, u32[]{:S(2)}) %collective-permute-start.48) | collective-permute-done | bytes 131104 | tf_op jit(solution)/shard_map/ppermute | solution.py:20
  158.3 7.9 %collective-permute-done.35 = bf16[256,1024]{1,0:T(8,128)(2,1)S(1)} collective-permute-done((bf16[256,1024]{1,0:T(8,128)(2,1)S(1)}, bf16[256,1024]{1,0:T(8,128)(2,1)S(1)}, u32[]{:S(2)}, u32[]{:S(2)}) %collective-permute-start.35) | collective-permute-done | bytes 524320 | tf_op jit(solution)/shard_map/ppermute | solution.py:20
  167.9 2.6 %fusion.122 = (f32[1024]{0:T(1024)S(1)}, f32[1024]{0:T(1024)S(1)}, f32[256,1024]{1,0:T(8,128)S(1)}) fusion(f32[1024]{0:T(1024)S(1)} %bitcast.53, f32[256,1024]{1,0:T(8,128)S(1)} %copy-done, f32[1024]{0:T(1024)S(1)} %bitcast.50, f32[1024]{0:T(1024)S(1)} %convert_subtract_fusion, bf16[256,1024]{1,0:T(8,128)(2,1)} %get-tuple-element.38, ...), kind=kOutput, calls=%fused_computation.209 | convolution fusion | flops 542111744 | bytes 7360513 | tf_op jit(solution)/shard_map/dot_general | solution.py:15
  180.0 2.6 %collective-permute-done.52 = f32[2,1024]{1,0:T(2,128)S(1)} collective-permute-done((f32[2,1024]{1,0:T(2,128)S(1)}, f32[2,1024]{1,0:T(2,128)S(1)}, u32[]{:S(2)}, u32[]{:S(2)}) %collective-permute-start.52) | collective-permute-done | bytes 8224 | tf_op jit(solution)/shard_map/ppermute | solution.py:25
  187.2 4.0 %collective-permute-done.37 = bf16[128,512]{1,0:T(8,128)(2,1)S(1)} collective-permute-done((bf16[128,512]{1,0:T(8,128)(2,1)S(1)}, bf16[128,512]{1,0:T(8,128)(2,1)S(1)}, u32[]{:S(2)}, u32[]{:S(2)}) %collective-permute-start.37) | collective-permute-done | bytes 131104 | tf_op jit(solution)/shard_map/ppermute | solution.py:20
  211.8 3.0 %collective-permute-done.59 = bf16[32,1792]{1,0:T(8,128)(2,1)S(1)} collective-permute-done((bf16[32,1792]{1,0:T(8,128)(2,1)S(1)}, bf16[32,1792]{1,0:T(8,128)(2,1)S(1)}, u32[]{:S(2)}, u32[]{:S(2)}) %collective-permute-start.59) | collective-permute-done | bytes 114720 | tf_op jit(solution)/shard_map/ppermute | solution.py:20
  222.1 7.2 %collective-permute-start.65 = (f32[1]{0:T(128)}, f32[1]{0:T(128)}, u32[]{:S(2)}, u32[]{:S(2)}) collective-permute-start(f32[1]{0:T(128)} %add.262), channel_id=1, source_target_pairs={{0,1},{1,0},{2,3},{3,2},{4,5},{5,4},{6,7},{7,6},{8,9},{9,8},{10,11... | collective-permute-start | bytes 20 | tf_op jit(solution)/shard_map/ppermute | solution.py:25
  (235 shorter events, 104.5 us)
Async XLA Ops:
  42.1 15.2 %collective-permute-start.19 = (bf16[256,1024]{1,0:T(8,128)(2,1)}, bf16[256,1024]{1,0:T(8,128)(2,1)}, u32[]{:S(2)}, u32[]{:S(2)}) collective-permute-start(bf16[256,1024]{1,0:T(8,128)(2,1)} %get-tuple-element.38), channel_id=1, source_target_pairs={{0,8},{8,0},{16,24},{24,16},{1,9},{9,1},{17,25},{25,17},{2,10},{10... | collective-permute-start | bytes 1572872 | tf_op jit(solution)/shard_map/ppermute | solution.py:25
  45.9 16.5 %collective-permute-start.20 = (bf16[256,1024]{1,0:T(8,128)(2,1)}, bf16[256,1024]{1,0:T(8,128)(2,1)}, u32[]{:S(2)}, u32[]{:S(2)}) collective-permute-start(bf16[256,1024]{1,0:T(8,128)(2,1)} %get-tuple-element.38), channel_id=1, source_target_pairs={{0,4},{4,0},{1,5},{5,1},{2,6},{6,2},{3,7},{7,3},{8,12},{12,8},{9,1... | collective-permute-start | bytes 1572872 | tf_op jit(solution)/shard_map/ppermute | solution.py:20
  53.3 18.3 %collective-permute-start.30 = (bf16[256,1024]{1,0:T(8,128)(2,1)}, bf16[256,1024]{1,0:T(8,128)(2,1)S(1)}, u32[]{:S(2)}, u32[]{:S(2)}) collective-permute-start(bf16[256,1024]{1,0:T(8,128)(2,1)} %get-tuple-element.38), channel_id=1, source_target_pairs={{8,16},{16,8},{9,17},{17,9},{10,18},{18,10},{11,19},{19,11},{12,20... | collective-permute-start | bytes 1572872 | tf_op jit(solution)/shard_map/ppermute | solution.py:87
  61.1 26.8 %collective-permute-start.23 = (bf16[256,1024]{1,0:T(8,128)(2,1)S(1)}, bf16[256,1024]{1,0:T(8,128)(2,1)S(1)}, u32[]{:S(2)}, u32[]{:S(2)}) collective-permute-start(bf16[256,1024]{1,0:T(8,128)(2,1)S(1)} %get-tuple-element.36), channel_id=1, source_target_pairs={{8,16},{16,8},{9,17},{17,9},{10,18},{18,10},{11,19},{19,11},{12,20... | collective-permute-start | bytes 1572872 | tf_op jit(solution)/shard_map/ppermute | solution.py:87
  61.8 18.1 %collective-permute-start.13 = (bf16[256,1024]{1,0:T(8,128)(2,1)S(1)}, bf16[256,1024]{1,0:T(8,128)(2,1)S(1)}, u32[]{:S(2)}, u32[]{:S(2)}) collective-permute-start(bf16[256,1024]{1,0:T(8,128)(2,1)S(1)} %get-tuple-element.36), channel_id=1, source_target_pairs={{0,4},{4,0},{1,5},{5,1},{2,6},{6,2},{3,7},{7,3},{8,12},{12,8},{9,1... | collective-permute-start | bytes 1572872 | tf_op jit(solution)/shard_map/ppermute | solution.py:20
  71.5 16.3 %collective-permute-start.12 = (bf16[256,1024]{1,0:T(8,128)(2,1)S(1)}, bf16[256,1024]{1,0:T(8,128)(2,1)S(1)}, u32[]{:S(2)}, u32[]{:S(2)}) collective-permute-start(bf16[256,1024]{1,0:T(8,128)(2,1)S(1)} %get-tuple-element.36), channel_id=1, source_target_pairs={{0,8},{8,0},{16,24},{24,16},{1,9},{9,1},{17,25},{25,17},{2,10},{10... | collective-permute-start | bytes 1572872 | tf_op jit(solution)/shard_map/ppermute | solution.py:25
  71.6 28.1 %collective-permute-start.32 = (bf16[256,1024]{1,0:T(8,128)(2,1)}, bf16[256,1024]{1,0:T(8,128)(2,1)S(1)}, u32[]{:S(2)}, u32[]{:S(2)}) collective-permute-start(bf16[256,1024]{1,0:T(8,128)(2,1)} %collective-permute-done.19), channel_id=1, source_target_pairs={{8,16},{16,8},{9,17},{17,9},{10,18},{18,10},{11,19},{19,11},{12,20... | collective-permute-start | bytes 1572872 | tf_op jit(solution)/shard_map/ppermute | solution.py:88
  76.6 22.5 %collective-permute-start.31 = (bf16[256,1024]{1,0:T(8,128)(2,1)S(1)}, bf16[256,1024]{1,0:T(8,128)(2,1)S(1)}, u32[]{:S(2)}, u32[]{:S(2)}) collective-permute-start(bf16[256,1024]{1,0:T(8,128)(2,1)S(1)} %collective-permute-done.30), channel_id=1, source_target_pairs={{8,0},{16,24},{9,1},{17,25},{10,2},{18,26},{11,3},{19,27},{12,4},{... | collective-permute-start | bytes 1572872 | tf_op jit(solution)/shard_map/ppermute | solution.py:89
  79.9 27.9 %collective-permute-start.41 = (f32[128,1024]{1,0:T(8,128)S(1)}, f32[128,1024]{1,0:T(8,128)S(1)}, u32[]{:S(2)}, u32[]{:S(2)}) collective-permute-start(f32[128,1024]{1,0:T(8,128)S(1)} %constant_dynamic-slice_fusion.6), channel_id=1, source_target_pairs={{0,2},{2,0},{1,3},{3,1},{4,6},{6,4},{5,7},{7,5},{8,10},{10,8},{9,1... | collective-permute-start | bytes 1572872 | tf_op jit(solution)/shard_map/ppermute | solution.py:25
  87.8 16.9 %collective-permute-start.15 = (bf16[128,1024]{1,0:T(8,128)(2,1)S(1)}, bf16[128,1024]{1,0:T(8,128)(2,1)S(1)}, u32[]{:S(2)}, u32[]{:S(2)}) collective-permute-start(bf16[128,1024]{1,0:T(8,128)(2,1)S(1)} %slice.37), channel_id=1, source_target_pairs={{0,8},{8,0},{16,24},{24,16},{1,9},{9,1},{17,25},{25,17},{2,10},{10... | collective-permute-start | bytes 786440 | tf_op jit(solution)/shard_map/ppermute | solution.py:25
  99.0 19.0 %collective-permute-start.25 = (bf16[256,1024]{1,0:T(8,128)(2,1)S(1)}, bf16[256,1024]{1,0:T(8,128)(2,1)S(1)}, u32[]{:S(2)}, u32[]{:S(2)}) collective-permute-start(bf16[256,1024]{1,0:T(8,128)(2,1)S(1)} %collective-permute-done.12), channel_id=1, source_target_pairs={{8,16},{16,8},{9,17},{17,9},{10,18},{18,10},{11,19},{19,11},{12,20... | collective-permute-start | bytes 1572872 | tf_op jit(solution)/shard_map/ppermute | solution.py:88
  99.7 16.8 %collective-permute-start.24 = (bf16[256,1024]{1,0:T(8,128)(2,1)S(1)}, bf16[256,1024]{1,0:T(8,128)(2,1)S(1)}, u32[]{:S(2)}, u32[]{:S(2)}) collective-permute-start(bf16[256,1024]{1,0:T(8,128)(2,1)S(1)} %collective-permute-done.23), channel_id=1, source_target_pairs={{8,0},{16,24},{9,1},{17,25},{10,2},{18,26},{11,3},{19,27},{12,4},{... | collective-permute-start | bytes 1572872 | tf_op jit(solution)/shard_map/ppermute | solution.py:89
  101.1 17.5 %collective-permute-start.33 = (bf16[256,1024]{1,0:T(8,128)(2,1)S(1)}, bf16[256,1024]{1,0:T(8,128)(2,1)S(1)}, u32[]{:S(2)}, u32[]{:S(2)}) collective-permute-start(bf16[256,1024]{1,0:T(8,128)(2,1)S(1)} %broadcast_select_fusion.2), channel_id=1, source_target_pairs={{0,4},{4,0},{1,5},{5,1},{2,6},{6,2},{3,7},{7,3},{8,12},{12,8},{9,1... | collective-permute-start | bytes 1572872 | tf_op jit(solution)/shard_map/ppermute | solution.py:20
  104.7 23.0 %collective-permute-start.39 = (bf16[256,1024]{1,0:T(8,128)(2,1)S(1)}, bf16[256,1024]{1,0:T(8,128)(2,1)S(1)}, u32[]{:S(2)}, u32[]{:S(2)}) collective-permute-start(bf16[256,1024]{1,0:T(8,128)(2,1)S(1)} %collective-permute-done.32), channel_id=1, source_target_pairs={{8,0},{16,24},{9,1},{17,25},{10,2},{18,26},{11,3},{19,27},{12,4},{... | collective-permute-start | bytes 1572872 | tf_op jit(solution)/shard_map/ppermute | solution.py:91
  107.8 15.2 %collective-permute-start.16 = (f32[128,1024]{1,0:T(8,128)S(1)}, f32[128,1024]{1,0:T(8,128)S(1)}, u32[]{:S(2)}, u32[]{:S(2)}) collective-permute-start(f32[128,1024]{1,0:T(8,128)S(1)} %constant_dynamic-slice_fusion.9), channel_id=1, source_target_pairs={{0,2},{2,0},{1,3},{3,1},{4,6},{6,4},{5,7},{7,5},{8,10},{10,8},{9,1... | collective-permute-start | bytes 1572872 | tf_op jit(solution)/shard_map/ppermute | solution.py:25
  118.1 18.3 %collective-permute-start.26 = (bf16[256,1024]{1,0:T(8,128)(2,1)S(1)}, bf16[256,1024]{1,0:T(8,128)(2,1)S(1)}, u32[]{:S(2)}, u32[]{:S(2)}) collective-permute-start(bf16[256,1024]{1,0:T(8,128)(2,1)S(1)} %broadcast_select_fusion.3), channel_id=1, source_target_pairs={{0,4},{4,0},{1,5},{5,1},{2,6},{6,2},{3,7},{7,3},{8,12},{12,8},{9,1... | collective-permute-start | bytes 1572872 | tf_op jit(solution)/shard_map/ppermute | solution.py:20
  118.6 31.6 %collective-permute-start.34 = (bf16[256,1024]{1,0:T(8,128)(2,1)S(1)}, bf16[256,1024]{1,0:T(8,128)(2,1)S(1)}, u32[]{:S(2)}, u32[]{:S(2)}) collective-permute-start(bf16[256,1024]{1,0:T(8,128)(2,1)S(1)} %collective-permute-done.25), channel_id=1, source_target_pairs={{8,0},{16,24},{9,1},{17,25},{10,2},{18,26},{11,3},{19,27},{12,4},{... | collective-permute-start | bytes 1572872 | tf_op jit(solution)/shard_map/ppermute | solution.py:91
  123.0 44.2 %collective-permute-start.43 = (bf16[128,1024]{1,0:T(8,128)(2,1)S(1)}, bf16[128,1024]{1,0:T(8,128)(2,1)S(1)}, u32[]{:S(2)}, u32[]{:S(2)}) collective-permute-start(bf16[128,1024]{1,0:T(8,128)(2,1)S(1)} %add_convert_fusion.2), channel_id=1, source_target_pairs={{0,2},{2,0},{1,3},{3,1},{4,6},{6,4},{5,7},{7,5},{8,10},{10,8},{9,1... | collective-permute-start | bytes 786440 | tf_op jit(solution)/shard_map/ppermute | solution.py:25
  136.1 16.4 %collective-permute-start.46 = (bf16[128,512]{1,0:T(8,128)(2,1)S(1)}, bf16[128,512]{1,0:T(8,128)(2,1)S(1)}, u32[]{:S(2)}, u32[]{:S(2)}) collective-permute-start(bf16[128,512]{1,0:T(8,128)(2,1)S(1)} %add_convert_fusion.5), channel_id=1, source_target_pairs={{0,2},{2,0},{1,3},{3,1},{4,6},{6,4},{5,7},{7,5},{8,10},{10,8},{9,1... | collective-permute-start | bytes 393224 | tf_op jit(solution)/shard_map/ppermute | solution.py:25
  136.3 56.9 %collective-permute-start.18 = (bf16[128,1024]{1,0:T(8,128)(2,1)S(1)}, bf16[128,1024]{1,0:T(8,128)(2,1)S(1)}, u32[]{:S(2)}, u32[]{:S(2)}) collective-permute-start(bf16[128,1024]{1,0:T(8,128)(2,1)S(1)} %add_convert_fusion.3), channel_id=1, source_target_pairs={{0,2},{2,0},{1,3},{3,1},{4,6},{6,4},{5,7},{7,5},{8,10},{10,8},{9,1... | collective-permute-start | bytes 786440 | tf_op jit(solution)/shard_map/ppermute | solution.py:25
  148.7 23.3 %collective-permute-start.27 = (f32[128,512]{1,0:T(8,128)S(1)}, f32[128,512]{1,0:T(8,128)S(1)}, u32[]{:S(2)}, u32[]{:S(2)}) collective-permute-start(f32[128,512]{1,0:T(8,128)S(1)} %constant_dynamic-slice_fusion.8), channel_id=1, source_target_pairs={{0,2},{2,0},{1,3},{3,1},{4,6},{6,4},{5,7},{7,5},{8,10},{10,8},{9,1... | collective-permute-start | bytes 786440 | tf_op jit(solution)/shard_map/ppermute | solution.py:25
  152.0 14.2 %collective-permute-start.35 = (bf16[256,1024]{1,0:T(8,128)(2,1)S(1)}, bf16[256,1024]{1,0:T(8,128)(2,1)S(1)}, u32[]{:S(2)}, u32[]{:S(2)}) collective-permute-start(bf16[256,1024]{1,0:T(8,128)(2,1)S(1)} %broadcast_select_fusion.1), channel_id=1, source_target_pairs={{0,4},{4,0},{1,5},{5,1},{2,6},{6,2},{3,7},{7,3},{8,12},{12,8},{9,1... | collective-permute-start | bytes 1572872 | tf_op jit(solution)/shard_map/ppermute | solution.py:20
  172.0 14.9 %collective-permute-start.28 = (bf16[128,512]{1,0:T(8,128)(2,1)S(1)}, bf16[128,512]{1,0:T(8,128)(2,1)S(1)}, u32[]{:S(2)}, u32[]{:S(2)}) collective-permute-start(bf16[128,512]{1,0:T(8,128)(2,1)S(1)} %fusion.97), channel_id=1, source_target_pairs={{0,1},{1,0},{2,3},{3,2},{4,5},{5,4},{6,7},{7,6},{8,9},{9,8},{10,11... | collective-permute-start | bytes 393224 | tf_op jit(solution)/shard_map/ppermute | solution.py:20
  217.0 14.0 %collective-permute-start.60 = (f32[128,1792]{1,0:T(8,128)S(1)}, f32[128,1792]{1,0:T(8,128)S(1)}, u32[]{:S(2)}, u32[]{:S(2)}) collective-permute-start(f32[128,1792]{1,0:T(8,128)S(1)} %constant_dynamic-slice_fusion.1), channel_id=1, source_target_pairs={{0,2},{2,0},{1,3},{3,1},{4,6},{6,4},{5,7},{7,5},{8,10},{10,8},{9,1... | collective-permute-start | bytes 2752520 | tf_op jit(solution)/shard_map/ppermute | solution.py:25
  (53 other events, 471.6 us)

commit v2 on v0

v2 whole, which is shorter than its diff:
```python
import jax
import jax.numpy as jnp
from jax import lax
from jax.sharding import Mesh
from jax.sharding import PartitionSpec as P

OFF_WEIGHT = 0.1
EPS = 1e-05
Z_CHIPS = 4
F32 = jnp.float32
BF16 = jnp.bfloat16


def dot(a, b, dims):
    return lax.dot_general(a, b, (dims, ((), ())), preferred_element_type=F32)


def shift(x, axis, step):
    size = lax.axis_size(axis)
    return lax.ppermute(x, axis, [(i, (i + step) % size) for i in range(size)])


def flip(x, axis, bit=1):
    size = lax.axis_size(axis)
    return lax.ppermute(x, axis, [(i, i ^ bit) for i in range(size)])


def cube_sum(x, *axes):
    for axis in axes:
        bit = 1
        while bit < lax.axis_size(axis):
            x = x + flip(x, axis, bit)
            bit *= 2
    return x


def own_block(x, index, count, axis):
    size = x.shape[axis] // count
    return lax.dynamic_slice_in_dim(x, index * size, size, axis)


def both_cores(x, axis=0):
    got = flip(x, "core")
    first = lax.axis_index("core") == 0
    return jnp.where(first, jnp.concatenate([x, got], axis), jnp.concatenate([got, x], axis))


def add_cores(x):
    core = lax.axis_index("core")
    return own_block(x, core, 2, 0) + flip(own_block(x, 1 - core, 2, 0), "core")


def weight_blocks(proj):
    num_feat = lax.axis_size("feat")
    feat = lax.axis_index("feat")
    cols = own_block(proj, lax.axis_index("core"), 2, 1)
    return [own_block(cols, (feat - step) % num_feat, num_feat, 0) for step in range(num_feat)]


def swap_feat(x):
    return [shift(x, "feat", step) for step in range(1, lax.axis_size("feat"))]


def moments(z_table, z_text):
    count = z_table.shape[0]
    mean_table, mean_text = jnp.mean(z_table, axis=0), jnp.mean(z_text, axis=0)
    centered_table, centered_text = z_table - mean_table, z_text - mean_text
    state = jnp.stack(
        [
            mean_table,
            mean_text,
            jnp.sum(centered_table * centered_table, axis=0),
            jnp.sum(centered_text * centered_text, axis=0),
            jnp.sum(centered_table * centered_text, axis=0),
        ]
    )
    for axis in ("z", "y"):
        bit = 1
        while bit < lax.axis_size(axis):
            other = flip(state, axis, bit)
            gap = state[:2] - other[:2]
            moved = (count / 2) * jnp.concatenate([gap * gap, gap[:1] * gap[1:]], 0)
            state = jnp.concatenate([(state[:2] + other[:2]) / 2, state[2:] + other[2:] + moved], 0)
            count *= 2
            bit *= 2
    return state[:2], state[2:] / count


def gather_rows(own):
    z = lax.axis_index("z")
    end = (z == 0) | (z == Z_CHIPS - 1)
    half = own.shape[0] // 2
    near = flip(own, "z")
    mid = lax.ppermute(own, "z", [(1, 2), (2, 1)])
    far_in = lax.ppermute(near, "z", [(1, 2), (2, 1)])
    far_end = lax.ppermute(mid, "z", [(1, 0), (2, 3)])
    far = jnp.where(end, far_end, far_in)
    last_end = lax.ppermute(far_in, "z", [(1, 0), (2, 3)])
    last = jnp.where(end, last_end, mid)
    early, late = [own, near, far], [last]
    for step in range(1, lax.axis_size("y")):
        y_own = shift(own, "y", step)
        y_near = [shift(near[:half], "y", step), flip(y_own[half:], "z")]
        early += [y_own, *y_near, shift(far, "y", step)]
        late += [shift(last, "y", step)]
    return jnp.concatenate(early, 0), jnp.concatenate(late, 0)


def gram_part(half, rows):
    return add_cores(dot(half, rows, ((1,), (1,))))


def add_feat(mine, others, axis):
    for other in others:
        mine = mine + other.astype(F32)
    return both_cores(mine.astype(BF16), axis)


def column_sums(d, normed):
    return jnp.stack([jnp.sum(d, axis=0), jnp.sum(d * normed, axis=0)])


def backward(d, normed, inverse, means):
    return (inverse * (d - means[0] - normed * means[1])).astype(BF16)


def swap_parts(sent):
    num_feat = lax.axis_size("feat")
    return [shift(part, "feat", num_feat - step) for step, part in enumerate(sent, 1)]


def body(table, text, table_proj, text_proj):
    pairs = table.shape[0] * 2 * lax.axis_size("z") * lax.axis_size("y")
    features = table_proj.shape[1] * lax.axis_size("feat")
    mine = jnp.stack([table, text])
    others = swap_feat(mine)
    weights = lax.optimization_barrier((weight_blocks(table_proj), weight_blocks(text_proj)))
    table_weights, text_weights = weights
    mine = both_cores(mine, 1)
    z_table = dot(mine[0], table_weights[0], ((1,), (0,)))
    z_text = dot(mine[1], text_weights[0], ((1,), (0,)))
    z_table, z_text, others = lax.optimization_barrier((z_table, z_text, others))
    for other, table_weight, text_weight in zip(others, table_weights[1:], text_weights[1:]):
        other = both_cores(other, 1)
        z_table = z_table + dot(other[0], table_weight, ((1,), (0,)))
        z_text = z_text + dot(other[1], text_weight, ((1,), (0,)))

    centers, spreads = moments(z_table, z_text)
    inverse_table, inverse_text = lax.rsqrt(spreads[0] + EPS), lax.rsqrt(spreads[1] + EPS)
    diag = inverse_table * inverse_text * spreads[2]
    diag_weight = (diag - 1.0).astype(BF16).astype(F32) - OFF_WEIGHT * diag
    normed_table = (z_table - centers[0]) * inverse_table
    normed_text = (z_text - centers[1]) * inverse_text
    half_table, half_text = normed_table.astype(BF16), normed_text.astype(BF16)
    all_table = gather_rows(half_table)
    all_text = gather_rows(half_text)

    gram_table = gram_part(half_table, all_table[0])
    others_table = swap_feat(gram_table.astype(BF16))
    early_text, late_text, late_table, others_table = lax.optimization_barrier(
        (all_text[0], all_text[1], all_table[1], others_table)
    )
    all_table, all_text = (all_table[0], late_table), (early_text, late_text)
    gram_text = gram_part(half_text, early_text)
    others_text = swap_feat(gram_text.astype(BF16))
    late = jnp.stack([gram_part(half_table, all_table[1]), gram_part(half_text, all_text[1])])
    late = add_feat(late, swap_feat(late.astype(BF16)), 1)
    gram_table = add_feat(gram_table, others_table, 0)
    gram_text = add_feat(gram_text, others_text, 0)
    grams = (gram_table, gram_text), late

    off_table, off_text = 0.0, 0.0
    for gram, rows_table, rows_text in zip(grams, all_table, all_text):
        off_table = off_table + dot(gram[1], rows_table, ((1,), (0,)))
        off_text = off_text + dot(gram[0], rows_text, ((1,), (0,)))
    d_table = (OFF_WEIGHT / pairs) * off_table + half_text.astype(F32) * diag_weight
    d_text = (OFF_WEIGHT / pairs) * off_text + half_table.astype(F32) * diag_weight
    sums = jnp.concatenate([column_sums(d_text, normed_text), column_sums(d_table, normed_table)], 0)
    means = cube_sum(sums, "z", "y") / pairs

    back_text = backward(d_text, normed_text, inverse_text, means[:2])
    parts_text = [dot(back_text, weight, ((1,), (1,))) for weight in text_weights[1:]]
    d_table, parts_text = lax.optimization_barrier((d_table, parts_text))
    sent_text = [add_cores(part).astype(BF16) for part in parts_text]
    back_table = backward(d_table, normed_table, inverse_table, means[2:])
    parts_table = [dot(back_table, weight, ((1,), (1,))) for weight in table_weights[1:]]
    sent_text, parts_table, back_text = lax.optimization_barrier((sent_text, parts_table, back_text))
    grads_text = swap_parts(sent_text)
    sent_table = [add_cores(part).astype(BF16) for part in parts_table]
    back_text, back_table, sent_table = lax.optimization_barrier((back_text, back_table, sent_table))
    own_text = dot(back_text, text_weights[0], ((1,), (1,)))
    sent_table, own_text, *grads_text = lax.optimization_barrier((sent_table, own_text, *grads_text))
    grads_table = swap_parts(sent_table)
    own_table = dot(back_table, table_weights[0], ((1,), (1,)))

    squares = means[3] - diag_weight * diag
    terms = (1.0 - diag) * (1.0 - diag) - OFF_WEIGHT * diag * diag + squares
    loss_part, own_table = lax.optimization_barrier((jnp.sum(terms).reshape(1), own_table))
    loss_total = cube_sum(loss_part, "core", "feat")
    grad_text = add_cores(own_text) + sum(part.astype(F32) for part in grads_text)
    grad_table = add_cores(own_table) + sum(part.astype(F32) for part in grads_table)
    return grad_table, grad_text, loss_total / features


def solution(mesh):
    devices = mesh.devices
    split = Mesh(
        devices.reshape(Z_CHIPS, devices.shape[0] // (2 * Z_CHIPS), 2, devices.shape[1]),
        ("z", "y", "core", "feat"),
    )
    rows = ("z", "y", "core")
    placed = (P(rows, "feat"), P(rows, "feat"), P(None, "feat"), P(None, "feat"))
    return jax.shard_map(
        body,
        mesh=split,
        in_specs=placed,
        out_specs=(P(rows, "feat"), P(rows, "feat"), P()),
        check_vma=False,
    )
```

time: 221 us -> 228 us (1.032)
  local copies, waits for them, and re-layouts: 8.84 us -> 31.5 us
  matrix products: 33 us -> 15.5 us
  starting transfers between devices: 67.1 us -> 53.2 us
  waiting for transfers between devices: 97.1 us -> 109 us
  other arithmetic: 9.24 us -> 13.2 us
    dynamic_slice x8 -> x10, local copies, waits for them, and re-layouts: 0.43 us -> 18.4 us  [own_block(): return lax.dynamic_slice_in_dim(x, index * size, size, axis)]
    dot_general x16, matrix products: 33 us -> 15.5 us  [dot(): return lax.dot_general(a, b, (dims, ((), ())), preferred_element_type=F32)]
    ppermute x16 -> x14, starting transfers between devices: 22 us -> 12.8 us  [shift(): return lax.ppermute(x, axis, [(i, (i + step) % size) for i in range(size)])]
    ppermute x16 -> x14, waiting for transfers between devices: 41.8 us -> 49 us  [shift(): return lax.ppermute(x, axis, [(i, (i + step) % size) for i in range(size)])]
    ppermute x34 -> x25, starting transfers between devices: 34.7 us -> 30 us  [flip(): return lax.ppermute(x, axis, [(i, i ^ bit) for i in range(size)])]
    unnamed x48 -> x38, local copies, waits for them, and re-layouts: 4.24 us -> 8.9 us
    ppermute x2, waiting for transfers between devices: 13.4 us -> 17.2 us  [gather_rows(): last_end = lax.ppermute(far_in, 'z', [(1, 0), (2, 3)])]
    ppermute x2, waiting for transfers between devices: 11.9 us -> 15.3 us  [gather_rows(): far_end = lax.ppermute(mid, 'z', [(1, 0), (2, 3)])]
  transfers between devices with their start and end apart: 58 -> 47, of which waited for: 26 -> 22; matrix products, arithmetic and copies ran while one was open for 21% -> 20% of each run, Pallas kernels for 0% -> 0%
where the time goes in v2:
time: 228 us; the launch traced here: 227 us
  waiting for transfers between devices  109 us (48%)
  starting transfers between devices  53.2 us (23%)
  local copies, waits for them, and re-layouts  31.5 us (14%)
  matrix products  15.5 us (7%)
  other arithmetic  13.2 us (6%)
  between operations  4.35 us (2%)
    ppermute x14, waiting for transfers between devices, shift(): return lax.ppermute(x, axis, [(i, (i + step) % size) for i in range(size)])  49 us
    ppermute x25, starting transfers between devices, flip(): return lax.ppermute(x, axis, [(i, i ^ bit) for i in range(size)])  30 us
    ppermute x25, waiting for transfers between devices, flip(): return lax.ppermute(x, axis, [(i, i ^ bit) for i in range(size)])  27.5 us
    dynamic_slice x10, local copies, waits for them, and re-layouts, own_block(): return lax.dynamic_slice_in_dim(x, index * size, size, axis)  18.4 us
    ppermute x2, waiting for transfers between devices, gather_rows(): last_end = lax.ppermute(far_in, 'z', [(1, 0), (2, 3)])  17.2 us
    dot_general x16, matrix products, dot(): return lax.dot_general(a, b, (dims, ((), ())), preferred_element_type=F32)  15.5 us
    ppermute x2, waiting for transfers between devices, gather_rows(): far_end = lax.ppermute(mid, 'z', [(1, 0), (2, 3)])  15.3 us
    ppermute x14, starting transfers between devices, shift(): return lax.ppermute(x, axis, [(i, (i + step) % size) for i in range(size)])  12.8 us
  transfers between devices with their start and end apart: 47, of which 22 were waited for; matrix products, arithmetic and copies ran while one was open for 20% of the time, Pallas kernels for 0%

profile of v2, /device:TPU:0, one launch (start us, length us, event | category | flops | bytes accessed | tf_op | source)
XLA Modules:
  0.0 226.9 jit_solution(18083410589428040204)
XLA Ops:
  2.4 2.6 %collective-permute-start.1 = (bf16[2,128,1792]{2,1,0:T(8,128)(2,1)S(1)}, bf16[2,128,1792]{2,1,0:T(8,128)(2,1)S(1)}, u32[]{:S(2)}, u32[]{:S(2)}) collective-permute-start(bf16[2,128,1792]{2,1,0:T(8,128)(2,1)S(1)} %pad_maximum_fusion.2), channel_id=1, source_target_pairs={{0,1},{1,0},{2,3},{3,2},{4,5},{5,4},{6,7},{7,6},{8,9},{9,8},{10,11... | collective-permute-start | bytes 2752520 | tf_op jit(solution)/shard_map/ppermute | solution.py:20
  5.0 10.6 %fusion.51 = (bf16[1792,1024]{1,0:T(8,128)(2,1)}, bf16[1792,1024]{1,0:T(8,128)(2,1)}) fusion(bf16[3584,2048]{1,0:T(8,128)(2,1)} %param.6, s32[]{:T(128)S(6)} %select_n.114, s32[]{:T(128)S(6)} %select_n.111, s32[]{:T(128)S(6)} %select_n.109), kind=kLoop, calls=%fused_computation.141 | loop fusion | bytes 14680076 | tf_op jit(solution)/shard_map/dynamic_slice | solution.py:39
  15.6 7.3 %fusion.50 = (bf16[1792,1024]{1,0:T(8,128)(2,1)}, bf16[1792,1024]{1,0:T(8,128)(2,1)}) fusion(bf16[3584,2048]{1,0:T(8,128)(2,1)S(1)} %copy-done.2, s32[]{:T(128)S(6)} %select_n.114, s32[]{:T(128)S(6)} %select_n.111, s32[]{:T(128)S(6)} %select_n.109), kind=kLoop, calls=%fused_computation.140 | loop fusion | bytes 14680076 | tf_op jit(solution)/shard_map/dynamic_slice | solution.py:39
  28.8 2.5 %collective-permute-done.2 = bf16[2,128,1792]{2,1,0:T(8,128)(2,1)S(1)} collective-permute-done((bf16[2,128,1792]{2,1,0:T(8,128)(2,1)S(1)}, bf16[2,128,1792]{2,1,0:T(8,128)(2,1)S(1)}, u32[]{:S(2)}, u32[]{:S(2)}) %collective-permute-start.2) | collective-permute-done | bytes 917536 | tf_op jit(solution)/shard_map/ppermute | solution.py:25
  37.7 2.3 %collective-permute-done.3 = f32[5,1024]{1,0:T(8,128)S(1)} collective-permute-done((f32[5,1024]{1,0:T(8,128)S(1)}, f32[5,1024]{1,0:T(8,128)S(1)}, u32[]{:S(2)}, u32[]{:S(2)}) %collective-permute-start.3) | collective-permute-done | bytes 20512 | tf_op jit(solution)/shard_map/ppermute | solution.py:25
  40.1 2.7 %collective-permute-start.4 = (f32[5,1024]{1,0:T(8,128)S(1)}, f32[5,1024]{1,0:T(8,128)S(1)}, u32[]{:S(2)}, u32[]{:S(2)}) collective-permute-start(f32[5,1024]{1,0:T(8,128)S(1)} %pad_maximum_fusion.4), channel_id=1, source_target_pairs={{0,16},{8,24},{16,0},{24,8},{1,17},{9,25},{17,1},{25,9},{2,18},{10... | collective-permute-start | bytes 61448 | tf_op jit(solution)/shard_map/ppermute | solution.py:25
  42.8 2.2 collective-permute-done.4
  46.6 2.4 %collective-permute-done.5 = f32[5,1024]{1,0:T(8,128)S(1)} collective-permute-done((f32[5,1024]{1,0:T(8,128)S(1)}, f32[5,1024]{1,0:T(8,128)S(1)}, u32[]{:S(2)}, u32[]{:S(2)}) %collective-permute-start.5) | collective-permute-done | bytes 20512 | tf_op jit(solution)/shard_map/ppermute | solution.py:25
  53.1 3.7 %collective-permute-start.6 = (bf16[256,1024]{1,0:T(8,128)(2,1)S(1)}, bf16[256,1024]{1,0:T(8,128)(2,1)}, u32[]{:S(2)}, u32[]{:S(2)}) collective-permute-start(bf16[256,1024]{1,0:T(8,128)(2,1)S(1)} %get-tuple-element.63), channel_id=1, source_target_pairs={{0,8},{8,0},{16,24},{24,16},{1,9},{9,1},{17,25},{25,17},{2,10},{10... | collective-permute-start | bytes 1572872 | tf_op jit(solution)/shard_map/ppermute | solution.py:25
  58.3 6.7 %collective-permute-done.10 = bf16[256,1024]{1,0:T(8,128)(2,1)S(1)} collective-permute-done((bf16[256,1024]{1,0:T(8,128)(2,1)S(1)}, bf16[256,1024]{1,0:T(8,128)(2,1)S(1)}, u32[]{:S(2)}, u32[]{:S(2)}) %collective-permute-start.10) | collective-permute-done | bytes 524320 | tf_op jit(solution)/shard_map/ppermute | solution.py:20
  73.4 5.0 %collective-permute-start.12 = (bf16[128,1024]{1,0:T(8,128)(2,1)S(1)}, bf16[128,1024]{1,0:T(8,128)(2,1)S(1)}, u32[]{:S(2)}, u32[]{:S(2)}) collective-permute-start(bf16[128,1024]{1,0:T(8,128)(2,1)S(1)} %slice.160), channel_id=1, source_target_pairs={{0,8},{8,0},{16,24},{24,16},{1,9},{9,1},{17,25},{25,17},{2,10},{10... | collective-permute-start | bytes 786440 | tf_op jit(solution)/shard_map/ppermute | solution.py:25
  86.3 5.9 %collective-permute-done.8 = bf16[256,1024]{1,0:T(8,128)(2,1)} collective-permute-done((bf16[256,1024]{1,0:T(8,128)(2,1)}, bf16[256,1024]{1,0:T(8,128)(2,1)}, u32[]{:S(2)}, u32[]{:S(2)}) %collective-permute-start.8) | collective-permute-done | bytes 524320 | tf_op jit(solution)/shard_map/ppermute | solution.py:96
  95.4 2.7 %collective-permute-start.21 = (bf16[128,1024]{1,0:T(8,128)(2,1)S(1)}, bf16[128,1024]{1,0:T(8,128)(2,1)S(1)}, u32[]{:S(2)}, u32[]{:S(2)}) collective-permute-start(bf16[128,1024]{1,0:T(8,128)(2,1)S(1)} %slice.163), channel_id=1, source_target_pairs={{0,8},{8,0},{16,24},{24,16},{1,9},{9,1},{17,25},{25,17},{2,10},{10... | collective-permute-start | bytes 786440 | tf_op jit(solution)/shard_map/ppermute | solution.py:25
  99.8 9.4 %collective-permute-done.17 = bf16[256,1024]{1,0:T(8,128)(2,1)S(1)} collective-permute-done((bf16[256,1024]{1,0:T(8,128)(2,1)}, bf16[256,1024]{1,0:T(8,128)(2,1)S(1)}, u32[]{:S(2)}, u32[]{:S(2)}) %collective-permute-start.17) | collective-permute-done | bytes 524320 | tf_op jit(solution)/shard_map/ppermute | solution.py:96
  115.2 17.2 %collective-permute-done.23 = bf16[256,1024]{1,0:T(8,128)(2,1)S(1)} collective-permute-done((bf16[256,1024]{1,0:T(8,128)(2,1)S(1)}, bf16[256,1024]{1,0:T(8,128)(2,1)S(1)}, u32[]{:S(2)}, u32[]{:S(2)}) %collective-permute-start.23) | collective-permute-done | bytes 524320 | tf_op jit(solution)/shard_map/ppermute | solution.py:98
  135.5 11.7 %collective-permute-done.24 = bf16[256,1024]{1,0:T(8,128)(2,1)S(1)} collective-permute-done((bf16[256,1024]{1,0:T(8,128)(2,1)S(1)}, bf16[256,1024]{1,0:T(8,128)(2,1)S(1)}, u32[]{:S(2)}, u32[]{:S(2)}) %collective-permute-start.24) | collective-permute-done | bytes 524320 | tf_op jit(solution)/shard_map/ppermute | solution.py:20
  147.3 5.5 %collective-permute-done.26 = bf16[256,1024]{1,0:T(8,128)(2,1)S(1)} collective-permute-done((bf16[256,1024]{1,0:T(8,128)(2,1)S(1)}, bf16[256,1024]{1,0:T(8,128)(2,1)S(1)}, u32[]{:S(2)}, u32[]{:S(2)}) %collective-permute-start.26) | collective-permute-done | bytes 524320 | tf_op jit(solution)/shard_map/ppermute | solution.py:20
  156.9 7.8 %collective-permute-done.31 = bf16[2,128,512]{2,1,0:T(8,128)(2,1)S(1)} collective-permute-done((bf16[2,128,512]{2,1,0:T(8,128)(2,1)S(1)}, bf16[2,128,512]{2,1,0:T(8,128)(2,1)S(1)}, u32[]{:S(2)}, u32[]{:S(2)}) %collective-permute-start.31) | collective-permute-done | bytes 262176 | tf_op jit(solution)/shard_map/ppermute | solution.py:20
  167.0 9.5 %collective-permute-done.34 = bf16[128,1536]{1,0:T(8,128)(2,1)S(1)} collective-permute-done((bf16[128,1536]{1,0:T(8,128)(2,1)S(1)}, bf16[128,1536]{1,0:T(8,128)(2,1)S(1)}, u32[]{:S(2)}, u32[]{:S(2)}) %collective-permute-start.34) | collective-permute-done | bytes 393248 | tf_op jit(solution)/shard_map/ppermute | solution.py:20
  181.1 2.4 %collective-permute-done.36 = f32[4,1024]{1,0:T(4,128)S(1)} collective-permute-done((f32[4,1024]{1,0:T(4,128)S(1)}, f32[4,1024]{1,0:T(4,128)S(1)}, u32[]{:S(2)}, u32[]{:S(2)}) %collective-permute-start.36) | collective-permute-done | bytes 16416 | tf_op jit(solution)/shard_map/ppermute | solution.py:25
  185.7 2.6 %collective-permute-done.37 = f32[4,1024]{1,0:T(4,128)S(1)} collective-permute-done((f32[4,1024]{1,0:T(4,128)S(1)}, f32[4,1024]{1,0:T(4,128)S(1)}, u32[]{:S(2)}, u32[]{:S(2)}) %collective-permute-start.37) | collective-permute-done | bytes 16416 | tf_op jit(solution)/shard_map/ppermute | solution.py:25
  188.9 3.3 %collective-permute-done.38 = f32[4,1024]{1,0:T(4,128)S(1)} collective-permute-done((f32[4,1024]{1,0:T(4,128)S(1)}, f32[4,1024]{1,0:T(4,128)S(1)}, u32[]{:S(2)}, u32[]{:S(2)}) %collective-permute-start.38) | collective-permute-done | bytes 16416 | tf_op jit(solution)/shard_map/ppermute | solution.py:25
  202.9 7.7 %collective-permute-done.42 = bf16[128,1792]{1,0:T(8,128)(2,1)S(1)} collective-permute-done((bf16[128,1792]{1,0:T(8,128)(2,1)S(1)}, bf16[128,1792]{1,0:T(8,128)(2,1)S(1)}, u32[]{:S(2)}, u32[]{:S(2)}) %collective-permute-start.42) | collective-permute-done | bytes 458784 | tf_op jit(solution)/shard_map/ppermute | solution.py:20
  214.9 6.0 %collective-permute-start.46 = (f32[1]{0:T(128)}, f32[1]{0:T(128)}, u32[]{:S(2)}, u32[]{:S(2)}) collective-permute-start(f32[1]{0:T(128)} %add.207), channel_id=1, source_target_pairs={{0,1},{1,0},{2,3},{3,2},{4,5},{5,4},{6,7},{7,6},{8,9},{9,8},{10,11... | collective-permute-start | bytes 20 | tf_op jit(solution)/shard_map/ppermute | solution.py:25
  (190 shorter events, 82.7 us)
Async XLA Ops:
  1.9 21.1 %collective-permute-start = (bf16[2,128,1792]{2,1,0:T(8,128)(2,1)S(1)}, bf16[2,128,1792]{2,1,0:T(8,128)(2,1)}, u32[]{:S(2)}, u32[]{:S(2)}) collective-permute-start(bf16[2,128,1792]{2,1,0:T(8,128)(2,1)S(1)} %pad_maximum_fusion.2), channel_id=1, source_target_pairs={{0,2},{2,0},{1,3},{3,1},{4,6},{6,4},{5,7},{7,5},{8,10},{10,8},{9,1... | collective-permute-start | bytes 2752520 | tf_op jit(solution)/shard_map/ppermute | solution.py:25
  2.4 26.3 %collective-permute-start.1 = (bf16[2,128,1792]{2,1,0:T(8,128)(2,1)S(1)}, bf16[2,128,1792]{2,1,0:T(8,128)(2,1)S(1)}, u32[]{:S(2)}, u32[]{:S(2)}) collective-permute-start(bf16[2,128,1792]{2,1,0:T(8,128)(2,1)S(1)} %pad_maximum_fusion.2), channel_id=1, source_target_pairs={{0,1},{1,0},{2,3},{3,2},{4,5},{5,4},{6,7},{7,6},{8,9},{9,8},{10,11... | collective-permute-start | bytes 2752520 | tf_op jit(solution)/shard_map/ppermute | solution.py:20
  50.1 14.9 %collective-permute-start.10 = (bf16[256,1024]{1,0:T(8,128)(2,1)S(1)}, bf16[256,1024]{1,0:T(8,128)(2,1)S(1)}, u32[]{:S(2)}, u32[]{:S(2)}) collective-permute-start(bf16[256,1024]{1,0:T(8,128)(2,1)S(1)} %get-tuple-element.63), channel_id=1, source_target_pairs={{0,4},{4,0},{1,5},{5,1},{2,6},{6,2},{3,7},{7,3},{8,12},{12,8},{9,1... | collective-permute-start | bytes 1572872 | tf_op jit(solution)/shard_map/ppermute | solution.py:20
  51.7 14.8 %collective-permute-start.7 = (bf16[256,1024]{1,0:T(8,128)(2,1)S(1)}, bf16[256,1024]{1,0:T(8,128)(2,1)}, u32[]{:S(2)}, u32[]{:S(2)}) collective-permute-start(bf16[256,1024]{1,0:T(8,128)(2,1)S(1)} %get-tuple-element.63), channel_id=1, source_target_pairs={{8,16},{16,8},{9,17},{17,9},{10,18},{18,10},{11,19},{19,11},{12,20... | collective-permute-start | bytes 1572872 | tf_op jit(solution)/shard_map/ppermute | solution.py:94
  53.1 16.6 %collective-permute-start.6 = (bf16[256,1024]{1,0:T(8,128)(2,1)S(1)}, bf16[256,1024]{1,0:T(8,128)(2,1)}, u32[]{:S(2)}, u32[]{:S(2)}) collective-permute-start(bf16[256,1024]{1,0:T(8,128)(2,1)S(1)} %get-tuple-element.63), channel_id=1, source_target_pairs={{0,8},{8,0},{16,24},{24,16},{1,9},{9,1},{17,25},{25,17},{2,10},{10... | collective-permute-start | bytes 1572872 | tf_op jit(solution)/shard_map/ppermute | solution.py:25
  57.8 15.6 %collective-permute-start.19 = (bf16[256,1024]{1,0:T(8,128)(2,1)S(1)}, bf16[256,1024]{1,0:T(8,128)(2,1)}, u32[]{:S(2)}, u32[]{:S(2)}) collective-permute-start(bf16[256,1024]{1,0:T(8,128)(2,1)S(1)} %get-tuple-element.67), channel_id=1, source_target_pairs={{0,4},{4,0},{1,5},{5,1},{2,6},{6,2},{3,7},{7,3},{8,12},{12,8},{9,1... | collective-permute-start | bytes 1572872 | tf_op jit(solution)/shard_map/ppermute | solution.py:20
  58.3 22.7 %collective-permute-start.15 = (bf16[256,1024]{1,0:T(8,128)(2,1)S(1)}, bf16[256,1024]{1,0:T(8,128)(2,1)}, u32[]{:S(2)}, u32[]{:S(2)}) collective-permute-start(bf16[256,1024]{1,0:T(8,128)(2,1)S(1)} %get-tuple-element.67), channel_id=1, source_target_pairs={{0,8},{8,0},{16,24},{24,16},{1,9},{9,1},{17,25},{25,17},{2,10},{10... | collective-permute-start | bytes 1572872 | tf_op jit(solution)/shard_map/ppermute | solution.py:25
  65.0 20.6 %collective-permute-start.16 = (bf16[256,1024]{1,0:T(8,128)(2,1)S(1)}, bf16[256,1024]{1,0:T(8,128)(2,1)}, u32[]{:S(2)}, u32[]{:S(2)}) collective-permute-start(bf16[256,1024]{1,0:T(8,128)(2,1)S(1)} %get-tuple-element.67), channel_id=1, source_target_pairs={{8,16},{16,8},{9,17},{17,9},{10,18},{18,10},{11,19},{19,11},{12,20... | collective-permute-start | bytes 1572872 | tf_op jit(solution)/shard_map/ppermute | solution.py:94
  66.5 25.7 %collective-permute-start.8 = (bf16[256,1024]{1,0:T(8,128)(2,1)}, bf16[256,1024]{1,0:T(8,128)(2,1)}, u32[]{:S(2)}, u32[]{:S(2)}) collective-permute-start(bf16[256,1024]{1,0:T(8,128)(2,1)} %collective-permute-done.7), channel_id=1, source_target_pairs={{8,0},{16,24},{9,1},{17,25},{10,2},{18,26},{11,3},{19,27},{12,4},{... | collective-permute-start | bytes 1572872 | tf_op jit(solution)/shard_map/ppermute | solution.py:96
  69.8 23.8 %collective-permute-start.9 = (bf16[256,1024]{1,0:T(8,128)(2,1)}, bf16[256,1024]{1,0:T(8,128)(2,1)}, u32[]{:S(2)}, u32[]{:S(2)}) collective-permute-start(bf16[256,1024]{1,0:T(8,128)(2,1)} %collective-permute-done.6), channel_id=1, source_target_pairs={{8,16},{16,8},{9,17},{17,9},{10,18},{18,10},{11,19},{19,11},{12,20... | collective-permute-start | bytes 1572872 | tf_op jit(solution)/shard_map/ppermute | solution.py:95
  73.4 24.8 %collective-permute-start.12 = (bf16[128,1024]{1,0:T(8,128)(2,1)S(1)}, bf16[128,1024]{1,0:T(8,128)(2,1)S(1)}, u32[]{:S(2)}, u32[]{:S(2)}) collective-permute-start(bf16[128,1024]{1,0:T(8,128)(2,1)S(1)} %slice.160), channel_id=1, source_target_pairs={{0,8},{8,0},{16,24},{24,16},{1,9},{9,1},{17,25},{25,17},{2,10},{10... | collective-permute-start | bytes 786440 | tf_op jit(solution)/shard_map/ppermute | solution.py:25
  85.6 24.9 %collective-permute-start.18 = (bf16[256,1024]{1,0:T(8,128)(2,1)}, bf16[256,1024]{1,0:T(8,128)(2,1)S(1)}, u32[]{:S(2)}, u32[]{:S(2)}) collective-permute-start(bf16[256,1024]{1,0:T(8,128)(2,1)} %collective-permute-done.15), channel_id=1, source_target_pairs={{8,16},{16,8},{9,17},{17,9},{10,18},{18,10},{11,19},{19,11},{12,20... | collective-permute-start | bytes 1572872 | tf_op jit(solution)/shard_map/ppermute | solution.py:95
  92.2 17.0 %collective-permute-start.17 = (bf16[256,1024]{1,0:T(8,128)(2,1)}, bf16[256,1024]{1,0:T(8,128)(2,1)S(1)}, u32[]{:S(2)}, u32[]{:S(2)}) collective-permute-start(bf16[256,1024]{1,0:T(8,128)(2,1)} %collective-permute-done.16), channel_id=1, source_target_pairs={{8,0},{16,24},{9,1},{17,25},{10,2},{18,26},{11,3},{19,27},{12,4},{... | collective-permute-start | bytes 1572872 | tf_op jit(solution)/shard_map/ppermute | solution.py:96
  94.8 17.4 %collective-permute-start.13 = (bf16[256,1024]{1,0:T(8,128)(2,1)S(1)}, bf16[256,1024]{1,0:T(8,128)(2,1)S(1)}, u32[]{:S(2)}, u32[]{:S(2)}) collective-permute-start(bf16[256,1024]{1,0:T(8,128)(2,1)S(1)} %get-tuple-element.61), channel_id=1, source_target_pairs={{0,4},{4,0},{1,5},{5,1},{2,6},{6,2},{3,7},{7,3},{8,12},{12,8},{9,1... | collective-permute-start | bytes 1572872 | tf_op jit(solution)/shard_map/ppermute | solution.py:20
  95.4 19.7 %collective-permute-start.21 = (bf16[128,1024]{1,0:T(8,128)(2,1)S(1)}, bf16[128,1024]{1,0:T(8,128)(2,1)S(1)}, u32[]{:S(2)}, u32[]{:S(2)}) collective-permute-start(bf16[128,1024]{1,0:T(8,128)(2,1)S(1)} %slice.163), channel_id=1, source_target_pairs={{0,8},{8,0},{16,24},{24,16},{1,9},{9,1},{17,25},{25,17},{2,10},{10... | collective-permute-start | bytes 786440 | tf_op jit(solution)/shard_map/ppermute | solution.py:25
  98.2 16.4 %collective-permute-start.20 = (bf16[128,1024]{1,0:T(8,128)(2,1)S(1)}, bf16[128,1024]{1,0:T(8,128)(2,1)S(1)}, u32[]{:S(2)}, u32[]{:S(2)}) collective-permute-start(bf16[128,1024]{1,0:T(8,128)(2,1)S(1)} %slice.162), channel_id=1, source_target_pairs={{0,4},{4,0},{1,5},{5,1},{2,6},{6,2},{3,7},{7,3},{8,12},{12,8},{9,1... | collective-permute-start | bytes 786440 | tf_op jit(solution)/shard_map/ppermute | solution.py:20
  109.2 23.9 %collective-permute-start.25 = (bf16[256,1024]{1,0:T(8,128)(2,1)}, bf16[256,1024]{1,0:T(8,128)(2,1)S(1)}, u32[]{:S(2)}, u32[]{:S(2)}) collective-permute-start(bf16[256,1024]{1,0:T(8,128)(2,1)} %collective-permute-done.9), channel_id=1, source_target_pairs={{8,0},{16,24},{9,1},{17,25},{10,2},{18,26},{11,3},{19,27},{12,4},{... | collective-permute-start | bytes 1572872 | tf_op jit(solution)/shard_map/ppermute | solution.py:98
  110.5 22.0 %collective-permute-start.23 = (bf16[256,1024]{1,0:T(8,128)(2,1)S(1)}, bf16[256,1024]{1,0:T(8,128)(2,1)S(1)}, u32[]{:S(2)}, u32[]{:S(2)}) collective-permute-start(bf16[256,1024]{1,0:T(8,128)(2,1)S(1)} %collective-permute-done.18), channel_id=1, source_target_pairs={{8,0},{16,24},{9,1},{17,25},{10,2},{18,26},{11,3},{19,27},{12,4},{... | collective-permute-start | bytes 1572872 | tf_op jit(solution)/shard_map/ppermute | solution.py:98
  113.4 21.4 %collective-permute-start.14 = (f32[128,1536]{1,0:T(8,128)S(1)}, f32[128,1536]{1,0:T(8,128)S(1)}, u32[]{:S(2)}, u32[]{:S(2)}) collective-permute-start(f32[128,1536]{1,0:T(8,128)S(1)} %constant_dynamic-slice_fusion.7), channel_id=1, source_target_pairs={{0,2},{2,0},{1,3},{3,1},{4,6},{6,4},{5,7},{7,5},{8,10},{10,8},{9,1... | collective-permute-start | bytes 2359304 | tf_op jit(solution)/shard_map/ppermute | solution.py:25
  114.6 20.9 %collective-permute-start.22 = (bf16[256,1024]{1,0:T(8,128)(2,1)S(1)}, bf16[256,1024]{1,0:T(8,128)(2,1)S(1)}, u32[]{:S(2)}, u32[]{:S(2)}) collective-permute-start(bf16[256,1024]{1,0:T(8,128)(2,1)S(1)} %get-tuple-element.65), channel_id=1, source_target_pairs={{0,4},{4,0},{1,5},{5,1},{2,6},{6,2},{3,7},{7,3},{8,12},{12,8},{9,1... | collective-permute-start | bytes 1572872 | tf_op jit(solution)/shard_map/ppermute | solution.py:20
  133.2 19.7 %collective-permute-start.26 = (bf16[256,1024]{1,0:T(8,128)(2,1)S(1)}, bf16[256,1024]{1,0:T(8,128)(2,1)S(1)}, u32[]{:S(2)}, u32[]{:S(2)}) collective-permute-start(bf16[256,1024]{1,0:T(8,128)(2,1)S(1)} %broadcast_select_fusion), channel_id=1, source_target_pairs={{0,4},{4,0},{1,5},{5,1},{2,6},{6,2},{3,7},{7,3},{8,12},{12,8},{9,1... | collective-permute-start | bytes 1572872 | tf_op jit(solution)/shard_map/ppermute | solution.py:20
  134.8 18.1 %collective-permute-start.27 = (bf16[128,1536]{1,0:T(8,128)(2,1)S(1)}, bf16[128,1536]{1,0:T(8,128)(2,1)S(1)}, u32[]{:S(2)}, u32[]{:S(2)}) collective-permute-start(bf16[128,1536]{1,0:T(8,128)(2,1)S(1)} %fusion.23), channel_id=1, source_target_pairs={{0,1},{1,0},{2,3},{3,2},{4,5},{5,4},{6,7},{7,6},{8,9},{9,8},{10,11... | collective-permute-start | bytes 1179656 | tf_op jit(solution)/shard_map/ppermute | solution.py:20
  156.6 20.1 %collective-permute-start.28 = (bf16[128,1536]{1,0:T(8,128)(2,1)S(1)}, bf16[128,1536]{1,0:T(8,128)(2,1)S(1)}, u32[]{:S(2)}, u32[]{:S(2)}) collective-permute-start(bf16[128,1536]{1,0:T(8,128)(2,1)S(1)} %add_convert_fusion.3), channel_id=1, source_target_pairs={{0,2},{2,0},{1,3},{3,1},{4,6},{6,4},{5,7},{7,5},{8,10},{10,8},{9,1... | collective-permute-start | bytes 1179656 | tf_op jit(solution)/shard_map/ppermute | solution.py:25
  201.0 22.6 %collective-permute-start.41 = (f32[128,1792]{1,0:T(8,128)S(1)}, f32[128,1792]{1,0:T(8,128)S(1)}, u32[]{:S(2)}, u32[]{:S(2)}) collective-permute-start(f32[128,1792]{1,0:T(8,128)S(1)} %constant_dynamic-slice_fusion.1), channel_id=1, source_target_pairs={{0,2},{2,0},{1,3},{3,1},{4,6},{6,4},{5,7},{7,5},{8,10},{10,8},{9,1... | collective-permute-start | bytes 2752520 | tf_op jit(solution)/shard_map/ppermute | solution.py:25
  (38 other events, 275.2 us)

commit v3 on v2

--- a/solution.py
+++ b/solution.py
@@ -86,24 +86,13 @@
     return state[:2], state[2:] / count
 
 
-def gather_rows(own):
+def at_end(end, inner):
     z = lax.axis_index("z")
-    end = (z == 0) | (z == Z_CHIPS - 1)
-    half = own.shape[0] // 2
-    near = flip(own, "z")
-    mid = lax.ppermute(own, "z", [(1, 2), (2, 1)])
-    far_in = lax.ppermute(near, "z", [(1, 2), (2, 1)])
-    far_end = lax.ppermute(mid, "z", [(1, 0), (2, 3)])
-    far = jnp.where(end, far_end, far_in)
-    last_end = lax.ppermute(far_in, "z", [(1, 0), (2, 3)])
-    last = jnp.where(end, last_end, mid)
-    early, late = [own, near, far], [last]
-    for step in range(1, lax.axis_size("y")):
-        y_own = shift(own, "y", step)
-        y_near = [shift(near[:half], "y", step), flip(y_own[half:], "z")]
-        early += [y_own, *y_near, shift(far, "y", step)]
-        late += [shift(last, "y", step)]
-    return jnp.concatenate(early, 0), jnp.concatenate(late, 0)
+    return jnp.where((z == 0) | (z == Z_CHIPS - 1), end, inner)
+
+
+def over_y(x):
+    return [flip(x, "y", step) for step in range(1, lax.axis_size("y"))]
 
 
 def gram_part(half, rows):
@@ -152,22 +141,35 @@
     normed_table = (z_table - centers[0]) * inverse_table
     normed_text = (z_text - centers[1]) * inverse_text
     half_table, half_text = normed_table.astype(BF16), normed_text.astype(BF16)
-    all_table = gather_rows(half_table)
-    all_text = gather_rows(half_text)
-
-    gram_table = gram_part(half_table, all_table[0])
+
+    half = jnp.stack([half_table, half_text])
+    near, mid, y_own = lax.optimization_barrier((flip(half, "z"), lax.ppermute(half, "z", [(1, 2), (2, 1)]), over_y(half)))
+    far_in, far_end, y_near = lax.optimization_barrier(
+        (lax.ppermute(near, "z", [(1, 2), (2, 1)]), lax.ppermute(mid, "z", [(1, 0), (2, 3)]), over_y(near))
+    )
+    far = at_end(far_end, far_in)
+    last_end, y_far = lax.optimization_barrier((lax.ppermute(far_in, "z", [(1, 0), (2, 3)]), over_y(far)))
+    last = at_end(last_end, mid)
+    cut = half.shape[1] // 2
+    y_last = over_y(last[:, :cut])
+    y_flip = [flip(block[:, cut:], "z") for block in y_far]
+
+    early = [half, near, far, *y_own, *y_near, *y_far]
+    early_table, early_text = [jnp.concatenate([block[i] for block in early], 0) for i in range(2)]
+    gram_table = gram_part(half_table, early_table)
     others_table = swap_feat(gram_table.astype(BF16))
-    early_text, late_text, late_table, others_table = lax.optimization_barrier(
-        (all_text[0], all_text[1], all_table[1], others_table)
-    )
-    all_table, all_text = (all_table[0], late_table), (early_text, late_text)
     gram_text = gram_part(half_text, early_text)
-    others_text = swap_feat(gram_text.astype(BF16))
-    late = jnp.stack([gram_part(half_table, all_table[1]), gram_part(half_text, all_text[1])])
-    late = add_feat(late, swap_feat(late.astype(BF16)), 1)
+    y_last, y_flip, others_table, gram_text = lax.optimization_barrier((y_last, y_flip, others_table, gram_text))
+    late = [last] + [block for pair in zip(y_last, y_flip) for block in pair]
+    late_table, late_text = [jnp.concatenate([block[i] for block in late], 0) for i in range(2)]
+    all_table, all_text = (early_table, late_table), (early_text, late_text)
+    parts = [gram_part(half_table, late_table), gram_text, gram_part(half_text, late_text)]
+    rest = jnp.concatenate(parts, 1)
+    rest = add_feat(rest, swap_feat(rest.astype(BF16)), 0)
     gram_table = add_feat(gram_table, others_table, 0)
-    gram_text = add_feat(gram_text, others_text, 0)
-    grams = (gram_table, gram_text), late
+    cuts = [late_table.shape[0], late_table.shape[0] + early_text.shape[0]]
+    late_gram, *gram_text = jnp.split(rest, cuts, 1)
+    grams = (gram_table, gram_text[0]), (late_gram, gram_text[1])
 
     off_table, off_text = 0.0, 0.0
     for gram, rows_table, rows_text in zip(grams, all_table, all_text):
@@ -198,6 +200,7 @@
     loss_part, own_table = lax.optimization_barrier((jnp.sum(terms).reshape(1), own_table))
     loss_total = cube_sum(loss_part, "core", "feat")
     grad_text = add_cores(own_text) + sum(part.astype(F32) for part in grads_text)
+    grad_text, *grads_table = lax.optimization_barrier((grad_text, *grads_table))
     grad_table = add_cores(own_table) + sum(part.astype(F32) for part in grads_table)
     return grad_table, grad_text, loss_total / features
 

time: 228 us -> 226 us (level)
  starting transfers between devices: 53.2 us -> 44.7 us
  waiting for transfers between devices: 109 us -> 113 us
    ppermute x25 -> x26, waiting for transfers between devices: 27.5 us -> 65.7 us  [flip(): return lax.ppermute(x, axis, [(i, i ^ bit) for i in range(size)])]
    ppermute x14 -> x5, waiting for transfers between devices: 49 us -> 26.3 us  [shift(): return lax.ppermute(x, axis, [(i, (i + step) % size) for i in range(size)])]
    ppermute x8 -> x4, waiting for transfers between devices: 32.5 us -> 20.9 us  [the longest x1 18.8 us: body(): lax.ppermute(mid, 'z', [(1, 0), (2, 3)])]
    ppermute x14 -> x5, starting transfers between devices: 12.8 us -> 4.8 us  [shift(): return lax.ppermute(x, axis, [(i, (i + step) % size) for i in range(size)])]
    ppermute x8 -> x4, starting transfers between devices: 10.4 us -> 6.12 us  [the longest x1 1.68 us: body(): lax.ppermute(half, 'z', [(1, 2), (2, 1)])]
    slice x4 -> x2, local copies, waits for them, and re-layouts: 4.07 us -> 0.07 us  [the longest x1 0.04 us: body(): y_flip = [flip(block[:, cut:], 'z') for block in y_far]]
    ppermute x25 -> x26, starting transfers between devices: 30 us -> 33.8 us  [flip(): return lax.ppermute(x, axis, [(i, i ^ bit) for i in range(size)])]
    unnamed x38 -> x30, local copies, waits for them, and re-layouts: 8.9 us -> 11.7 us
  transfers between devices with their start and end apart: 47 -> 35, of which waited for: 22 -> 22; matrix products, arithmetic and copies ran while one was open for 20% -> 18% of each run, Pallas kernels for 0% -> 0%
where the time goes in v3:
time: 226 us
  waiting for transfers between devices  113 us (50%)
  starting transfers between devices  44.7 us (20%)
  local copies, waits for them, and re-layouts  31.3 us (14%)
  matrix products  17.4 us (8%)
  other arithmetic  15.1 us (7%)
  between operations  4.32 us (2%)
    ppermute x26, waiting for transfers between devices, flip(): return lax.ppermute(x, axis, [(i, i ^ bit) for i in range(size)])  65.7 us
    ppermute x26, starting transfers between devices, flip(): return lax.ppermute(x, axis, [(i, i ^ bit) for i in range(size)])  33.8 us
    ppermute x5, waiting for transfers between devices, shift(): return lax.ppermute(x, axis, [(i, (i + step) % size) for i in range(size)])  26.3 us
    ppermute x1, waiting for transfers between devices, body(): lax.ppermute(mid, 'z', [(1, 0), (2, 3)])  18.8 us
    dynamic_slice x10, local copies, waits for them, and re-layouts, own_block(): return lax.dynamic_slice_in_dim(x, index * size, size, axis)  18.5 us
    dot_general x16, matrix products, dot(): return lax.dot_general(a, b, (dims, ((), ())), preferred_element_type=F32)  17.4 us
    unnamed x30, local copies, waits for them, and re-layouts  11.7 us
    ppermute x5, starting transfers between devices, shift(): return lax.ppermute(x, axis, [(i, (i + step) % size) for i in range(size)])  4.8 us
  transfers between devices with their start and end apart: 35, of which 22 were waited for; matrix products, arithmetic and copies ran while one was open for 18% of the time, Pallas kernels for 0%

profile of v3, /device:TPU:0, one launch (start us, length us, event | category | flops | bytes accessed | tf_op | source)
XLA Modules:
  0.0 225.6 jit_solution(4513010433888237505)
XLA Ops:
  0.6 2.2 pad_maximum_fusion.4
  3.2 2.5 %collective-permute-start.1 = (bf16[2,128,1792]{2,1,0:T(8,128)(2,1)}, bf16[2,128,1792]{2,1,0:T(8,128)(2,1)}, u32[]{:S(2)}, u32[]{:S(2)}) collective-permute-start(bf16[2,128,1792]{2,1,0:T(8,128)(2,1)} %pad_maximum_fusion.4), channel_id=1, source_target_pairs={{0,1},{1,0},{2,3},{3,2},{4,5},{5,4},{6,7},{7,6},{8,9},{9,8},{10,11... | collective-permute-start | bytes 2752520 | tf_op jit(solution)/shard_map/ppermute | solution.py:20
  5.7 10.7 %fusion.53 = (bf16[1792,1024]{1,0:T(8,128)(2,1)}, bf16[1792,1024]{1,0:T(8,128)(2,1)}) fusion(bf16[3584,2048]{1,0:T(8,128)(2,1)} %param.7, s32[]{:T(128)S(6)} %select_n.102, s32[]{:T(128)S(6)} %select_n.99, s32[]{:T(128)S(6)} %select_n.97), kind=kLoop, calls=%fused_computation.142 | loop fusion | bytes 14680076 | tf_op jit(solution)/shard_map/dynamic_slice | solution.py:39
  16.4 7.3 %fusion.54 = (bf16[1792,1024]{1,0:T(8,128)(2,1)}, bf16[1792,1024]{1,0:T(8,128)(2,1)}) fusion(bf16[3584,2048]{1,0:T(8,128)(2,1)S(1)} %copy-done.2, s32[]{:T(128)S(6)} %select_n.102, s32[]{:T(128)S(6)} %select_n.99, s32[]{:T(128)S(6)} %select_n.97), kind=kLoop, calls=%fused_computation.143 | loop fusion | bytes 14680076 | tf_op jit(solution)/shard_map/dynamic_slice | solution.py:39
  29.6 2.7 %collective-permute-done.2 = bf16[2,128,1792]{2,1,0:T(8,128)(2,1)S(1)} collective-permute-done((bf16[2,128,1792]{2,1,0:T(8,128)(2,1)}, bf16[2,128,1792]{2,1,0:T(8,128)(2,1)S(1)}, u32[]{:S(2)}, u32[]{:S(2)}) %collective-permute-start.2) | collective-permute-done | bytes 917536 | tf_op jit(solution)/shard_map/ppermute | solution.py:25
  39.9 2.3 %collective-permute-done.3 = f32[5,1024]{1,0:T(8,128)S(1)} collective-permute-done((f32[5,1024]{1,0:T(8,128)S(1)}, f32[5,1024]{1,0:T(8,128)S(1)}, u32[]{:S(2)}, u32[]{:S(2)}) %collective-permute-start.3) | collective-permute-done | bytes 20512 | tf_op jit(solution)/shard_map/ppermute | solution.py:25
  42.3 2.7 %collective-permute-start.4 = (f32[5,1024]{1,0:T(8,128)S(1)}, f32[5,1024]{1,0:T(8,128)S(1)}, u32[]{:S(2)}, u32[]{:S(2)}) collective-permute-start(f32[5,1024]{1,0:T(8,128)S(1)} %pad_maximum_fusion.9), channel_id=1, source_target_pairs={{0,16},{8,24},{16,0},{24,8},{1,17},{9,25},{17,1},{25,9},{2,18},{10... | collective-permute-start | bytes 61448 | tf_op jit(solution)/shard_map/ppermute | solution.py:25
  45.0 2.2 collective-permute-done.4
  48.9 2.4 %collective-permute-done.5 = f32[5,1024]{1,0:T(8,128)S(1)} collective-permute-done((f32[5,1024]{1,0:T(8,128)S(1)}, f32[5,1024]{1,0:T(8,128)S(1)}, u32[]{:S(2)}, u32[]{:S(2)}) %collective-permute-start.5) | collective-permute-done | bytes 20512 | tf_op jit(solution)/shard_map/ppermute | solution.py:25
  58.3 17.1 %collective-permute-done.6 = bf16[2,256,1024]{2,1,0:T(8,128)(2,1)} collective-permute-done((bf16[2,256,1024]{2,1,0:T(8,128)(2,1)S(1)}, bf16[2,256,1024]{2,1,0:T(8,128)(2,1)}, u32[]{:S(2)}, u32[]{:S(2)}) %collective-permute-start.6) | collective-permute-done | bytes 1048608 | tf_op jit(solution)/shard_map/ppermute | solution.py:25
  75.4 3.2 %collective-permute-done.8 = bf16[2,256,1024]{2,1,0:T(8,128)(2,1)} collective-permute-done((bf16[2,256,1024]{2,1,0:T(8,128)(2,1)S(1)}, bf16[2,256,1024]{2,1,0:T(8,128)(2,1)}, u32[]{:S(2)}, u32[]{:S(2)}) %collective-permute-start.8) | collective-permute-done | bytes 1048608 | tf_op jit(solution)/shard_map/ppermute | solution.py:25
  83.1 18.8 %collective-permute-done.10 = bf16[2,256,1024]{2,1,0:T(8,128)(2,1)} collective-permute-done((bf16[2,256,1024]{2,1,0:T(8,128)(2,1)}, bf16[2,256,1024]{2,1,0:T(8,128)(2,1)}, u32[]{:S(2)}, u32[]{:S(2)}) %collective-permute-start.10) | collective-permute-done | bytes 1048608 | tf_op jit(solution)/shard_map/ppermute | solution.py:148
  113.4 11.0 %collective-permute-done.13 = bf16[2,256,1024]{2,1,0:T(8,128)(2,1)S(1)} collective-permute-done((bf16[2,256,1024]{2,1,0:T(8,128)(2,1)S(1)}, bf16[2,256,1024]{2,1,0:T(8,128)(2,1)S(1)}, u32[]{:S(2)}, u32[]{:S(2)}) %collective-permute-start.13) | collective-permute-done | bytes 1048608 | tf_op jit(solution)/shard_map/ppermute | solution.py:25
  124.4 2.1 collective-permute-done.12
  127.4 2.9 %fusion.58 = f32[256,1536]{1,0:T(8,128)S(1)} fusion(bf16[256,1024]{1,0:T(8,128)(2,1)S(1)} %get-tuple-element.81, bf16[1536,1024]{1,0:T(8,128)(2,1)} %get-tuple-element.100), kind=kOutput, calls=%fused_computation.147 | convolution fusion | flops 805306368 | bytes 5242880 | tf_op jit(solution)/shard_map/dot_general | solution.py:15
  132.9 4.5 %collective-permute-start.16 = (bf16[2,128,1024]{2,1,0:T(8,128)(2,1)S(1)}, bf16[2,128,1024]{2,1,0:T(8,128)(2,1)S(1)}, u32[]{:S(2)}, u32[]{:S(2)}) collective-permute-start(bf16[2,128,1024]{2,1,0:T(8,128)(2,1)S(1)} %slice.171), channel_id=1, source_target_pairs={{0,8},{8,0},{16,24},{24,16},{1,9},{9,1},{17,25},{25,17},{2,10},{10... | collective-permute-start | bytes 1572872 | tf_op jit(solution)/shard_map/ppermute | solution.py:25
  138.3 7.9 %collective-permute-done.15 = bf16[2,128,1024]{2,1,0:T(8,128)(2,1)S(1)} collective-permute-done((bf16[2,128,1024]{2,1,0:T(8,128)(2,1)S(1)}, bf16[2,128,1024]{2,1,0:T(8,128)(2,1)S(1)}, u32[]{:S(2)}, u32[]{:S(2)}) %collective-permute-start.15) | collective-permute-done | bytes 524320 | tf_op jit(solution)/shard_map/ppermute | solution.py:25
  146.2 3.0 %collective-permute-done.16 = bf16[2,128,1024]{2,1,0:T(8,128)(2,1)S(1)} collective-permute-done((bf16[2,128,1024]{2,1,0:T(8,128)(2,1)S(1)}, bf16[2,128,1024]{2,1,0:T(8,128)(2,1)S(1)}, u32[]{:S(2)}, u32[]{:S(2)}) %collective-permute-start.16) | collective-permute-done | bytes 524320 | tf_op jit(solution)/shard_map/ppermute | solution.py:25
  152.8 16.5 %collective-permute-done.22 = bf16[128,2560]{1,0:T(8,128)(2,1)S(1)} collective-permute-done((bf16[128,2560]{1,0:T(8,128)(2,1)S(1)}, bf16[128,2560]{1,0:T(8,128)(2,1)S(1)}, u32[]{:S(2)}, u32[]{:S(2)}) %collective-permute-start.22) | collective-permute-done | bytes 655392 | tf_op jit(solution)/shard_map/ppermute | solution.py:20
  179.7 2.2 collective-permute-start.25
  181.9 2.5 %collective-permute-done.25 = f32[4,1024]{1,0:T(4,128)S(1)} collective-permute-done((f32[4,1024]{1,0:T(4,128)S(1)}, f32[4,1024]{1,0:T(4,128)S(1)}, u32[]{:S(2)}, u32[]{:S(2)}) %collective-permute-start.25) | collective-permute-done | bytes 16416 | tf_op jit(solution)/shard_map/ppermute | solution.py:25
  186.1 2.2 collective-permute-done.26
  197.0 9.8 %collective-permute-done.30 = bf16[128,1792]{1,0:T(8,128)(2,1)S(1)} collective-permute-done((bf16[128,1792]{1,0:T(8,128)(2,1)S(1)}, bf16[128,1792]{1,0:T(8,128)(2,1)S(1)}, u32[]{:S(2)}, u32[]{:S(2)}) %collective-permute-start.30) | collective-permute-done | bytes 458784 | tf_op jit(solution)/shard_map/ppermute | solution.py:20
  212.0 7.7 %collective-permute-start.34 = (f32[1]{0:T(128)}, f32[1]{0:T(128)}, u32[]{:S(2)}, u32[]{:S(2)}) collective-permute-start(f32[1]{0:T(128)} %add.203), channel_id=1, source_target_pairs={{0,1},{1,0},{2,3},{3,2},{4,5},{5,4},{6,7},{7,6},{8,9},{9,8},{10,11... | collective-permute-start | bytes 20 | tf_op jit(solution)/shard_map/ppermute | solution.py:25
  (154 shorter events, 75.0 us)
Async XLA Ops:
  2.8 21.0 %collective-permute-start = (bf16[2,128,1792]{2,1,0:T(8,128)(2,1)}, bf16[2,128,1792]{2,1,0:T(8,128)(2,1)}, u32[]{:S(2)}, u32[]{:S(2)}) collective-permute-start(bf16[2,128,1792]{2,1,0:T(8,128)(2,1)} %pad_maximum_fusion.4), channel_id=1, source_target_pairs={{0,2},{2,0},{1,3},{3,1},{4,6},{6,4},{5,7},{7,5},{8,10},{10,8},{9,1... | collective-permute-start | bytes 2752520 | tf_op jit(solution)/shard_map/ppermute | solution.py:25
  3.2 26.3 %collective-permute-start.1 = (bf16[2,128,1792]{2,1,0:T(8,128)(2,1)}, bf16[2,128,1792]{2,1,0:T(8,128)(2,1)}, u32[]{:S(2)}, u32[]{:S(2)}) collective-permute-start(bf16[2,128,1792]{2,1,0:T(8,128)(2,1)} %pad_maximum_fusion.4), channel_id=1, source_target_pairs={{0,1},{1,0},{2,3},{3,2},{4,5},{5,4},{6,7},{7,6},{8,9},{9,8},{10,11... | collective-permute-start | bytes 2752520 | tf_op jit(solution)/shard_map/ppermute | solution.py:20
  42.3 4.9 %collective-permute-start.4 = (f32[5,1024]{1,0:T(8,128)S(1)}, f32[5,1024]{1,0:T(8,128)S(1)}, u32[]{:S(2)}, u32[]{:S(2)}) collective-permute-start(f32[5,1024]{1,0:T(8,128)S(1)} %pad_maximum_fusion.9), channel_id=1, source_target_pairs={{0,16},{8,24},{16,0},{24,8},{1,17},{9,25},{17,1},{25,9},{2,18},{10... | collective-permute-start | bytes 61448 | tf_op jit(solution)/shard_map/ppermute | solution.py:25
  53.4 21.9 %collective-permute-start.6 = (bf16[2,256,1024]{2,1,0:T(8,128)(2,1)S(1)}, bf16[2,256,1024]{2,1,0:T(8,128)(2,1)}, u32[]{:S(2)}, u32[]{:S(2)}) collective-permute-start(bf16[2,256,1024]{2,1,0:T(8,128)(2,1)S(1)} %pad_maximum_fusion.1), channel_id=1, source_target_pairs={{0,8},{8,0},{16,24},{24,16},{1,9},{9,1},{17,25},{25,17},{2,10},{10... | collective-permute-start | bytes 3145736 | tf_op jit(solution)/shard_map/ppermute | solution.py:25
  55.1 20.3 %collective-permute-start.7 = (bf16[2,256,1024]{2,1,0:T(8,128)(2,1)S(1)}, bf16[2,256,1024]{2,1,0:T(8,128)(2,1)}, u32[]{:S(2)}, u32[]{:S(2)}) collective-permute-start(bf16[2,256,1024]{2,1,0:T(8,128)(2,1)S(1)} %pad_maximum_fusion.1), channel_id=1, source_target_pairs={{8,16},{16,8},{9,17},{17,9},{10,18},{18,10},{11,19},{19,11},{12,20... | collective-permute-start | bytes 3145736 | tf_op jit(solution)/shard_map/ppermute | solution.py:146
  56.8 21.8 %collective-permute-start.8 = (bf16[2,256,1024]{2,1,0:T(8,128)(2,1)S(1)}, bf16[2,256,1024]{2,1,0:T(8,128)(2,1)}, u32[]{:S(2)}, u32[]{:S(2)}) collective-permute-start(bf16[2,256,1024]{2,1,0:T(8,128)(2,1)S(1)} %pad_maximum_fusion.1), channel_id=1, source_target_pairs={{0,4},{4,0},{1,5},{5,1},{2,6},{6,2},{3,7},{7,3},{8,12},{12,8},{9,1... | collective-permute-start | bytes 3145736 | tf_op jit(solution)/shard_map/ppermute | solution.py:25
  78.5 23.3 %collective-permute-start.10 = (bf16[2,256,1024]{2,1,0:T(8,128)(2,1)}, bf16[2,256,1024]{2,1,0:T(8,128)(2,1)}, u32[]{:S(2)}, u32[]{:S(2)}) collective-permute-start(bf16[2,256,1024]{2,1,0:T(8,128)(2,1)} %collective-permute-done.7), channel_id=1, source_target_pairs={{8,0},{16,24},{9,1},{17,25},{10,2},{18,26},{11,3},{19,27},{12,4},{... | collective-permute-start | bytes 3145736 | tf_op jit(solution)/shard_map/ppermute | solution.py:148
  79.8 22.0 %collective-permute-start.11 = (bf16[2,256,1024]{2,1,0:T(8,128)(2,1)}, bf16[2,256,1024]{2,1,0:T(8,128)(2,1)}, u32[]{:S(2)}, u32[]{:S(2)}) collective-permute-start(bf16[2,256,1024]{2,1,0:T(8,128)(2,1)} %collective-permute-done.6), channel_id=1, source_target_pairs={{0,4},{4,0},{1,5},{5,1},{2,6},{6,2},{3,7},{7,3},{8,12},{12,8},{9,1... | collective-permute-start | bytes 3145736 | tf_op jit(solution)/shard_map/ppermute | solution.py:25
  81.4 20.5 %collective-permute-start.9 = (bf16[2,256,1024]{2,1,0:T(8,128)(2,1)}, bf16[2,256,1024]{2,1,0:T(8,128)(2,1)}, u32[]{:S(2)}, u32[]{:S(2)}) collective-permute-start(bf16[2,256,1024]{2,1,0:T(8,128)(2,1)} %collective-permute-done.6), channel_id=1, source_target_pairs={{8,16},{16,8},{9,17},{17,9},{10,18},{18,10},{11,19},{19,11},{12,20... | collective-permute-start | bytes 3145736 | tf_op jit(solution)/shard_map/ppermute | solution.py:148
  101.9 24.7 %collective-permute-start.12 = (bf16[2,256,1024]{2,1,0:T(8,128)(2,1)}, bf16[2,256,1024]{2,1,0:T(8,128)(2,1)S(1)}, u32[]{:S(2)}, u32[]{:S(2)}) collective-permute-start(bf16[2,256,1024]{2,1,0:T(8,128)(2,1)} %collective-permute-done.9), channel_id=1, source_target_pairs={{8,0},{16,24},{9,1},{17,25},{10,2},{18,26},{11,3},{19,27},{12,4},{... | collective-permute-start | bytes 3145736 | tf_op jit(solution)/shard_map/ppermute | solution.py:151
  104.7 19.7 %collective-permute-start.13 = (bf16[2,256,1024]{2,1,0:T(8,128)(2,1)S(1)}, bf16[2,256,1024]{2,1,0:T(8,128)(2,1)S(1)}, u32[]{:S(2)}, u32[]{:S(2)}) collective-permute-start(bf16[2,256,1024]{2,1,0:T(8,128)(2,1)S(1)} %broadcast_select_fusion.1), channel_id=1, source_target_pairs={{0,4},{4,0},{1,5},{5,1},{2,6},{6,2},{3,7},{7,3},{8,12},{12,8},{9,1... | collective-permute-start | bytes 3145736 | tf_op jit(solution)/shard_map/ppermute | solution.py:25
  131.4 6.0 %collective-permute-start.14 = (f32[128,1536]{1,0:T(8,128)S(1)}, f32[128,1536]{1,0:T(8,128)S(1)}, u32[]{:S(2)}, u32[]{:S(2)}) collective-permute-start(f32[128,1536]{1,0:T(8,128)S(1)} %constant_dynamic-slice_fusion.7), channel_id=1, source_target_pairs={{0,2},{2,0},{1,3},{3,1},{4,6},{6,4},{5,7},{7,5},{8,10},{10,8},{9,1... | collective-permute-start | bytes 2359304 | tf_op jit(solution)/shard_map/ppermute | solution.py:25
  131.5 6.6 %collective-permute-start.18 = (f32[128,1536]{1,0:T(8,128)S(1)}, f32[128,1536]{1,0:T(8,128)S(1)}, u32[]{:S(2)}, u32[]{:S(2)}) collective-permute-start(f32[128,1536]{1,0:T(8,128)S(1)} %constant_dynamic-slice_fusion.6), channel_id=1, source_target_pairs={{0,2},{2,0},{1,3},{3,1},{4,6},{6,4},{5,7},{7,5},{8,10},{10,8},{9,1... | collective-permute-start | bytes 2359304 | tf_op jit(solution)/shard_map/ppermute | solution.py:25
  132.3 13.9 %collective-permute-start.15 = (bf16[2,128,1024]{2,1,0:T(8,128)(2,1)S(1)}, bf16[2,128,1024]{2,1,0:T(8,128)(2,1)S(1)}, u32[]{:S(2)}, u32[]{:S(2)}) collective-permute-start(bf16[2,128,1024]{2,1,0:T(8,128)(2,1)S(1)} %slice.209), channel_id=1, source_target_pairs={{0,4},{4,0},{1,5},{5,1},{2,6},{6,2},{3,7},{7,3},{8,12},{12,8},{9,1... | collective-permute-start | bytes 1572872 | tf_op jit(solution)/shard_map/ppermute | solution.py:25
  132.9 16.3 %collective-permute-start.16 = (bf16[2,128,1024]{2,1,0:T(8,128)(2,1)S(1)}, bf16[2,128,1024]{2,1,0:T(8,128)(2,1)S(1)}, u32[]{:S(2)}, u32[]{:S(2)}) collective-permute-start(bf16[2,128,1024]{2,1,0:T(8,128)(2,1)S(1)} %slice.171), channel_id=1, source_target_pairs={{0,8},{8,0},{16,24},{24,16},{1,9},{9,1},{17,25},{25,17},{2,10},{10... | collective-permute-start | bytes 1572872 | tf_op jit(solution)/shard_map/ppermute | solution.py:25
  137.6 11.6 %collective-permute-start.17 = (bf16[128,1536]{1,0:T(8,128)(2,1)S(1)}, bf16[128,1536]{1,0:T(8,128)(2,1)S(1)}, u32[]{:S(2)}, u32[]{:S(2)}) collective-permute-start(bf16[128,1536]{1,0:T(8,128)(2,1)S(1)} %fusion.24), channel_id=1, source_target_pairs={{0,1},{1,0},{2,3},{3,2},{4,5},{5,4},{6,7},{7,6},{8,9},{9,8},{10,11... | collective-permute-start | bytes 1179656 | tf_op jit(solution)/shard_map/ppermute | solution.py:20
  152.2 17.1 %collective-permute-start.22 = (bf16[128,2560]{1,0:T(8,128)(2,1)S(1)}, bf16[128,2560]{1,0:T(8,128)(2,1)S(1)}, u32[]{:S(2)}, u32[]{:S(2)}) collective-permute-start(bf16[128,2560]{1,0:T(8,128)(2,1)S(1)} %fusion.4), channel_id=1, source_target_pairs={{0,1},{1,0},{2,3},{3,2},{4,5},{5,4},{6,7},{7,6},{8,9},{9,8},{10,11... | collective-permute-start | bytes 1966088 | tf_op jit(solution)/shard_map/ppermute | solution.py:20
  169.7 4.3 %collective-permute-start.19 = (bf16[128,1536]{1,0:T(8,128)(2,1)S(1)}, bf16[128,1536]{1,0:T(8,128)(2,1)S(1)}, u32[]{:S(2)}, u32[]{:S(2)}) collective-permute-start(bf16[128,1536]{1,0:T(8,128)(2,1)S(1)} %add_convert_fusion.3), channel_id=1, source_target_pairs={{0,2},{2,0},{1,3},{3,1},{4,6},{6,4},{5,7},{7,5},{8,10},{10,8},{9,1... | collective-permute-start | bytes 1179656 | tf_op jit(solution)/shard_map/ppermute | solution.py:25
  179.7 4.7 %collective-permute-start.25 = (f32[4,1024]{1,0:T(4,128)S(1)}, f32[4,1024]{1,0:T(4,128)S(1)}, u32[]{:S(2)}, u32[]{:S(2)}) collective-permute-start(f32[4,1024]{1,0:T(4,128)S(1)} %fusion.43), channel_id=1, source_target_pairs={{0,16},{8,24},{16,0},{24,8},{1,17},{9,25},{17,1},{25,9},{2,18},{10... | collective-permute-start | bytes 49160 | tf_op jit(solution)/shard_map/ppermute | solution.py:25
  193.8 12.9 %collective-permute-start.30 = (bf16[128,1792]{1,0:T(8,128)(2,1)S(1)}, bf16[128,1792]{1,0:T(8,128)(2,1)S(1)}, u32[]{:S(2)}, u32[]{:S(2)}) collective-permute-start(bf16[128,1792]{1,0:T(8,128)(2,1)S(1)} %add_convert_fusion.2), channel_id=1, source_target_pairs={{0,1},{1,0},{2,3},{3,2},{4,5},{5,4},{6,7},{7,6},{8,9},{9,8},{10,11... | collective-permute-start | bytes 1376264 | tf_op jit(solution)/shard_map/ppermute | solution.py:20
  206.8 15.5 %collective-permute-start.31 = (f32[128,1792]{1,0:T(8,128)S(1)}, f32[128,1792]{1,0:T(8,128)S(1)}, u32[]{:S(2)}, u32[]{:S(2)}) collective-permute-start(f32[128,1792]{1,0:T(8,128)S(1)} %constant_dynamic-slice_fusion), channel_id=1, source_target_pairs={{0,2},{2,0},{1,3},{3,1},{4,6},{6,4},{5,7},{7,5},{8,10},{10,8},{9,1... | collective-permute-start | bytes 2752520 | tf_op jit(solution)/shard_map/ppermute | solution.py:25
  208.2 15.2 %collective-permute-start.29 = (f32[128,1792]{1,0:T(8,128)S(1)}, f32[128,1792]{1,0:T(8,128)S(1)}, u32[]{:S(2)}, u32[]{:S(2)}) collective-permute-start(f32[128,1792]{1,0:T(8,128)S(1)} %constant_dynamic-slice_fusion.1), channel_id=1, source_target_pairs={{0,2},{2,0},{1,3},{3,1},{4,6},{6,4},{5,7},{7,5},{8,10},{10,8},{9,1... | collective-permute-start | bytes 2752520 | tf_op jit(solution)/shard_map/ppermute | solution.py:25
  208.8 14.6 %collective-permute-start.32 = (bf16[128,1792]{1,0:T(8,128)(2,1)S(1)}, bf16[128,1792]{1,0:T(8,128)(2,1)S(1)}, u32[]{:S(2)}, u32[]{:S(2)}) collective-permute-start(bf16[128,1792]{1,0:T(8,128)(2,1)S(1)} %add_convert_fusion.1), channel_id=1, source_target_pairs={{0,1},{1,0},{2,3},{3,2},{4,5},{5,4},{6,7},{7,6},{8,9},{9,8},{10,11... | collective-permute-start | bytes 1376264 | tf_op jit(solution)/shard_map/ppermute | solution.py:20
  212.0 9.6 %collective-permute-start.34 = (f32[1]{0:T(128)}, f32[1]{0:T(128)}, u32[]{:S(2)}, u32[]{:S(2)}) collective-permute-start(f32[1]{0:T(128)} %add.203), channel_id=1, source_target_pairs={{0,1},{1,0},{2,3},{3,2},{4,5},{5,4},{6,7},{7,6},{8,9},{9,8},{10,11... | collective-permute-start | bytes 20 | tf_op jit(solution)/shard_map/ppermute | solution.py:25
  (24 other events, 123.2 us)

commit v4 on v3

--- a/solution.py
+++ b/solution.py
@@ -1,6 +1,8 @@
 import jax
 import jax.numpy as jnp
 from jax import lax
+from jax.experimental import pallas as pl
+from jax.experimental.pallas import tpu as pltpu
 from jax.sharding import Mesh
 from jax.sharding import PartitionSpec as P
 
@@ -50,11 +52,38 @@
     return own_block(x, core, 2, 0) + flip(own_block(x, 1 - core, 2, 0), "core")
 
 
-def weight_blocks(proj):
+def cut_kernel(starts, *refs):
+    sources, blocks, sems = refs[:2], refs[2:-1], refs[-1]
+    count = len(blocks) // 2
+    rows, cols = blocks[0].shape
+    copies = []
+    for i, block in enumerate(blocks):
+        row = pl.multiple_of(starts[1 + i % count], 16)
+        col = pl.multiple_of(starts[0], 128)
+        source = sources[i // count].at[pl.ds(row, rows), pl.ds(col, cols)]
+        copies.append(pltpu.make_async_copy(source, block, sems.at[i]))
+    for copy in copies:
+        copy.start()
+    for copy in copies:
+        copy.wait()
+
+
+def weight_blocks(table_proj, text_proj):
     num_feat = lax.axis_size("feat")
     feat = lax.axis_index("feat")
-    cols = own_block(proj, lax.axis_index("core"), 2, 1)
-    return [own_block(cols, (feat - step) % num_feat, num_feat, 0) for step in range(num_feat)]
+    rows, cols = table_proj.shape[0] // num_feat, table_proj.shape[1] // 2
+    firsts = [(feat - step) % num_feat * rows for step in range(num_feat)]
+    starts = jnp.stack([lax.axis_index("core") * cols, *firsts]).astype(jnp.int32)
+    count = 2 * num_feat
+    blocks = pl.pallas_call(
+        cut_kernel,
+        out_shape=[jax.ShapeDtypeStruct((rows, cols), BF16)] * count,
+        in_specs=[pl.BlockSpec(memory_space=pltpu.SMEM), pl.BlockSpec(memory_space=pl.ANY), pl.BlockSpec(memory_space=pl.ANY)],
+        out_specs=[pl.BlockSpec(memory_space=pltpu.VMEM)] * count,
+        scratch_shapes=[pltpu.SemaphoreType.DMA((count,))],
+        compiler_params=pltpu.CompilerParams(vmem_limit_bytes=40 * 1024 * 1024),
+    )(starts, table_proj, text_proj)
+    return blocks[:num_feat], blocks[num_feat:]
 
 
 def swap_feat(x):
@@ -123,8 +152,7 @@
     features = table_proj.shape[1] * lax.axis_size("feat")
     mine = jnp.stack([table, text])
     others = swap_feat(mine)
-    weights = lax.optimization_barrier((weight_blocks(table_proj), weight_blocks(text_proj)))
-    table_weights, text_weights = weights
+    table_weights, text_weights = weight_blocks(table_proj, text_proj)
     mine = both_cores(mine, 1)
     z_table = dot(mine[0], table_weights[0], ((1,), (0,)))
     z_text = dot(mine[1], text_weights[0], ((1,), (0,)))
@@ -180,25 +208,26 @@
     sums = jnp.concatenate([column_sums(d_text, normed_text), column_sums(d_table, normed_table)], 0)
     means = cube_sum(sums, "z", "y") / pairs
 
+    squares = means[3] - diag_weight * diag
+    terms = (1.0 - diag) * (1.0 - diag) - OFF_WEIGHT * diag * diag + squares
+    loss_total = cube_sum(jnp.sum(terms).reshape(1), "feat")
+
     back_text = backward(d_text, normed_text, inverse_text, means[:2])
     parts_text = [dot(back_text, weight, ((1,), (1,))) for weight in text_weights[1:]]
     d_table, parts_text = lax.optimization_barrier((d_table, parts_text))
     sent_text = [add_cores(part).astype(BF16) for part in parts_text]
     back_table = backward(d_table, normed_table, inverse_table, means[2:])
     parts_table = [dot(back_table, weight, ((1,), (1,))) for weight in table_weights[1:]]
-    sent_text, parts_table, back_text = lax.optimization_barrier((sent_text, parts_table, back_text))
+    sent_text, parts_table, back_text, loss_total = lax.optimization_barrier((sent_text, parts_table, back_text, loss_total))
     grads_text = swap_parts(sent_text)
     sent_table = [add_cores(part).astype(BF16) for part in parts_table]
     back_text, back_table, sent_table = lax.optimization_barrier((back_text, back_table, sent_table))
+    grads_table = swap_parts(sent_table)
     own_text = dot(back_text, text_weights[0], ((1,), (1,)))
-    sent_table, own_text, *grads_text = lax.optimization_barrier((sent_table, own_text, *grads_text))
-    grads_table = swap_parts(sent_table)
+    loss_total = cube_sum(loss_total, "core")
+    back_table, *grads_text = lax.optimization_barrier((back_table, *grads_text))
     own_table = dot(back_table, table_weights[0], ((1,), (1,)))
 
-    squares = means[3] - diag_weight * diag
-    terms = (1.0 - diag) * (1.0 - diag) - OFF_WEIGHT * diag * diag + squares
-    loss_part, own_table = lax.optimization_barrier((jnp.sum(terms).reshape(1), own_table))
-    loss_total = cube_sum(loss_part, "core", "feat")
     grad_text = add_cores(own_text) + sum(part.astype(F32) for part in grads_text)
     grad_text, *grads_table = lax.optimization_barrier((grad_text, *grads_table))
     grad_table = add_cores(own_table) + sum(part.astype(F32) for part in grads_table)

time: 226 us -> 227 us (level)
  local copies, waits for them, and re-layouts: 31.3 us -> 10.3 us
  waiting for transfers between devices: 113 us -> 126 us
  Pallas kernels: 0 us -> 7.76 us
    dynamic_slice x10 -> x8, local copies, waits for them, and re-layouts: 18.5 us -> 0.45 us  [own_block(): return lax.dynamic_slice_in_dim(x, index * size, size, axis)]
    ppermute x5, waiting for transfers between devices: 26.3 us -> 43.8 us  [shift(): return lax.ppermute(x, axis, [(i, (i + step) % size) for i in range(size)])]
    pallas_call x0 -> x1, Pallas kernels: none -> 7.76 us  [weight_blocks(): pl.pallas_call(cut_kernel, out_shape=[jax.ShapeDtypeStruct((rows, cols),...]
    ppermute x26, waiting for transfers between devices: 65.7 us -> 61.3 us  [flip(): return lax.ppermute(x, axis, [(i, i ^ bit) for i in range(size)])]
    ppermute x5, starting transfers between devices: 4.8 us -> 8.76 us  [shift(): return lax.ppermute(x, axis, [(i, (i + step) % size) for i in range(size)])]
    ppermute x26, starting transfers between devices: 33.8 us -> 30.2 us  [flip(): return lax.ppermute(x, axis, [(i, i ^ bit) for i in range(size)])]
    unnamed x30 -> x28, local copies, waits for them, and re-layouts: 11.7 us -> 8.66 us
  transfers between devices with their start and end apart: 35 -> 35, of which waited for: 22 -> 24; matrix products, arithmetic and copies ran while one was open for 18% -> 10% of each run, Pallas kernels for 0% -> 3%
where the time goes in v4:
time: 227 us; the launch traced here: 226 us
  waiting for transfers between devices  126 us (56%)
  starting transfers between devices  45 us (20%)
  matrix products  17.4 us (8%)
  other arithmetic  15.2 us (7%)
  local copies, waits for them, and re-layouts  10.3 us (5%)
  Pallas kernels  7.76 us (3%)
  between operations  4.29 us (2%)
    ppermute x26, waiting for transfers between devices, flip(): return lax.ppermute(x, axis, [(i, i ^ bit) for i in range(size)])  61.3 us
    ppermute x5, waiting for transfers between devices, shift(): return lax.ppermute(x, axis, [(i, (i + step) % size) for i in range(size)])  43.8 us
    ppermute x26, starting transfers between devices, flip(): return lax.ppermute(x, axis, [(i, i ^ bit) for i in range(size)])  30.2 us
    ppermute x1, waiting for transfers between devices, body(): lax.ppermute(mid, 'z', [(1, 0), (2, 3)])  18.8 us
    dot_general x16, matrix products, dot(): return lax.dot_general(a, b, (dims, ((), ())), preferred_element_type=F32)  17.4 us
    ppermute x5, starting transfers between devices, shift(): return lax.ppermute(x, axis, [(i, (i + step) % size) for i in range(size)])  8.76 us
    unnamed x28, local copies, waits for them, and re-layouts  8.66 us
    pallas_call x1, Pallas kernels, weight_blocks(): pl.pallas_call(cut_kernel, out_shape=[jax.ShapeDtypeStruct((rows, cols),...  7.76 us
  transfers between devices with their start and end apart: 35, of which 24 were waited for; matrix products, arithmetic and copies ran while one was open for 10% of the time, Pallas kernels for 3%

profile of v4, /device:TPU:0, one launch (start us, length us, event | category | flops | bytes accessed | tf_op | source)
XLA Modules:
  0.0 226.0 jit_solution(20431595932370113)
XLA Ops:
  2.4 2.6 %collective-permute-start.1 = (bf16[2,128,1792]{2,1,0:T(8,128)(2,1)S(1)}, bf16[2,128,1792]{2,1,0:T(8,128)(2,1)}, u32[]{:S(2)}, u32[]{:S(2)}) collective-permute-start(bf16[2,128,1792]{2,1,0:T(8,128)(2,1)S(1)} %pad_maximum_fusion.4), channel_id=1, source_target_pairs={{0,1},{1,0},{2,3},{3,2},{4,5},{5,4},{6,7},{7,6},{8,9},{9,8},{10,11... | collective-permute-start | bytes 2752520 | tf_op jit(solution)/shard_map/ppermute | solution.py:22
  5.0 7.8 %shard_map.67 = (bf16[1792,1024]{1,0:T(8,128)(2,1)S(1)}, bf16[1792,1024]{1,0:T(8,128)(2,1)S(1)}, bf16[1792,1024]{1,0:T(8,128)(2,1)S(1)}, bf16[1792,1024]{1,0:T(8,128)(2,1)}) custom-call(s32[3]{0:T(128)S(1)} %pad_add_fusion.starts, bf16[3584,2048]{1,0:T(8,128)(2,1)} %refs_0_.1, bf16[3584,2048]{1,0:T(8,128)(2,1)} %refs_1_.1), custom_call_target="tpu_custom_call" | custom-call | tf_op jit(solution)/shard_map/pallas_call | solution.py:78
  12.9 3.1 %maximum_select_fusion = bf16[2,256,1792]{2,1,0:T(8,128)(2,1)S(1)} fusion(bf16[2,128,1792]{2,1,0:T(8,128)(2,1)} %collective-permute-done, bf16[1,128,1792]{2,1,0:T(8,128)(2,1)S(1)} %bitcast.98, bf16[1,128,1792]{2,1,0:T(8,128)(2,1)S(1)} %bitcast.100, pred[]{:T(512)S(6)} %eq.9), kind=kLoop, calls=%fused_computation | loop fusion | flops 11927552 | bytes 3670017 | tf_op jit(solution)/shard_map/jit(_where)/select_n | solution.py:47
  18.2 7.8 %collective-permute-done.1 = bf16[2,128,1792]{2,1,0:T(8,128)(2,1)} collective-permute-done((bf16[2,128,1792]{2,1,0:T(8,128)(2,1)S(1)}, bf16[2,128,1792]{2,1,0:T(8,128)(2,1)}, u32[]{:S(2)}, u32[]{:S(2)}) %collective-permute-start.1) | collective-permute-done | bytes 917536 | tf_op jit(solution)/shard_map/ppermute | solution.py:22
  26.0 2.7 %collective-permute-done.2 = bf16[2,128,1792]{2,1,0:T(8,128)(2,1)S(1)} collective-permute-done((bf16[2,128,1792]{2,1,0:T(8,128)(2,1)}, bf16[2,128,1792]{2,1,0:T(8,128)(2,1)S(1)}, u32[]{:S(2)}, u32[]{:S(2)}) %collective-permute-start.2) | collective-permute-done | bytes 917536 | tf_op jit(solution)/shard_map/ppermute | solution.py:27
  36.6 2.1 collective-permute-done.3
  38.7 2.9 %collective-permute-start.4 = (f32[5,1024]{1,0:T(8,128)S(1)}, f32[5,1024]{1,0:T(8,128)S(1)}, u32[]{:S(2)}, u32[]{:S(2)}) collective-permute-start(f32[5,1024]{1,0:T(8,128)S(1)} %pad_maximum_fusion.9), channel_id=1, source_target_pairs={{0,16},{8,24},{16,0},{24,8},{1,17},{9,25},{17,1},{25,9},{2,18},{10... | collective-permute-start | bytes 61448 | tf_op jit(solution)/shard_map/ppermute | solution.py:27
  45.5 2.1 collective-permute-done.5
  55.0 17.0 %collective-permute-done.6 = bf16[2,256,1024]{2,1,0:T(8,128)(2,1)} collective-permute-done((bf16[2,256,1024]{2,1,0:T(8,128)(2,1)S(1)}, bf16[2,256,1024]{2,1,0:T(8,128)(2,1)}, u32[]{:S(2)}, u32[]{:S(2)}) %collective-permute-start.6) | collective-permute-done | bytes 1048608 | tf_op jit(solution)/shard_map/ppermute | solution.py:27
  72.0 3.2 %collective-permute-done.8 = bf16[2,256,1024]{2,1,0:T(8,128)(2,1)} collective-permute-done((bf16[2,256,1024]{2,1,0:T(8,128)(2,1)S(1)}, bf16[2,256,1024]{2,1,0:T(8,128)(2,1)}, u32[]{:S(2)}, u32[]{:S(2)}) %collective-permute-start.8) | collective-permute-done | bytes 1048608 | tf_op jit(solution)/shard_map/ppermute | solution.py:27
  79.7 18.8 %collective-permute-done.10 = bf16[2,256,1024]{2,1,0:T(8,128)(2,1)} collective-permute-done((bf16[2,256,1024]{2,1,0:T(8,128)(2,1)}, bf16[2,256,1024]{2,1,0:T(8,128)(2,1)}, u32[]{:S(2)}, u32[]{:S(2)}) %collective-permute-start.10) | collective-permute-done | bytes 1048608 | tf_op jit(solution)/shard_map/ppermute | solution.py:176
  103.0 2.1 bitcast_dynamic-update-slice_fusion.3
  110.0 11.0 %collective-permute-done.13 = bf16[2,256,1024]{2,1,0:T(8,128)(2,1)S(1)} collective-permute-done((bf16[2,256,1024]{2,1,0:T(8,128)(2,1)S(1)}, bf16[2,256,1024]{2,1,0:T(8,128)(2,1)S(1)}, u32[]{:S(2)}, u32[]{:S(2)}) %collective-permute-start.13) | collective-permute-done | bytes 1048608 | tf_op jit(solution)/shard_map/ppermute | solution.py:27
  121.1 2.2 collective-permute-done.12
  124.1 2.9 %fusion.56 = f32[256,1536]{1,0:T(8,128)S(1)} fusion(bf16[256,1024]{1,0:T(8,128)(2,1)S(1)} %get-tuple-element.77, bf16[1536,1024]{1,0:T(8,128)(2,1)} %get-tuple-element.92), kind=kOutput, calls=%fused_computation.146 | convolution fusion | flops 805306368 | bytes 5242880 | tf_op jit(solution)/shard_map/dot_general | solution.py:17
  129.6 4.4 %collective-permute-start.15 = (bf16[2,128,1024]{2,1,0:T(8,128)(2,1)S(1)}, bf16[2,128,1024]{2,1,0:T(8,128)(2,1)S(1)}, u32[]{:S(2)}, u32[]{:S(2)}) collective-permute-start(bf16[2,128,1024]{2,1,0:T(8,128)(2,1)S(1)} %slice.166), channel_id=1, source_target_pairs={{0,8},{8,0},{16,24},{24,16},{1,9},{9,1},{17,25},{25,17},{2,10},{10... | collective-permute-start | bytes 1572872 | tf_op jit(solution)/shard_map/ppermute | solution.py:27
  135.9 7.0 %collective-permute-done.14 = bf16[2,128,1024]{2,1,0:T(8,128)(2,1)S(1)} collective-permute-done((bf16[2,128,1024]{2,1,0:T(8,128)(2,1)S(1)}, bf16[2,128,1024]{2,1,0:T(8,128)(2,1)S(1)}, u32[]{:S(2)}, u32[]{:S(2)}) %collective-permute-start.14) | collective-permute-done | bytes 524320 | tf_op jit(solution)/shard_map/ppermute | solution.py:27
  142.9 2.9 %collective-permute-done.15 = bf16[2,128,1024]{2,1,0:T(8,128)(2,1)S(1)} collective-permute-done((bf16[2,128,1024]{2,1,0:T(8,128)(2,1)S(1)}, bf16[2,128,1024]{2,1,0:T(8,128)(2,1)S(1)}, u32[]{:S(2)}, u32[]{:S(2)}) %collective-permute-start.15) | collective-permute-done | bytes 524320 | tf_op jit(solution)/shard_map/ppermute | solution.py:27
  150.5 15.5 %collective-permute-done.21 = bf16[128,2560]{1,0:T(8,128)(2,1)S(1)} collective-permute-done((bf16[128,2560]{1,0:T(8,128)(2,1)S(1)}, bf16[128,2560]{1,0:T(8,128)(2,1)S(1)}, u32[]{:S(2)}, u32[]{:S(2)}) %collective-permute-start.21) | collective-permute-done | bytes 655392 | tf_op jit(solution)/shard_map/ppermute | solution.py:22
  176.4 2.2 collective-permute-start.25
  178.6 2.5 %collective-permute-done.25 = f32[4,1024]{1,0:T(4,128)S(1)} collective-permute-done((f32[4,1024]{1,0:T(4,128)S(1)}, f32[4,1024]{1,0:T(4,128)S(1)}, u32[]{:S(2)}, u32[]{:S(2)}) %collective-permute-start.25) | collective-permute-done | bytes 16416 | tf_op jit(solution)/shard_map/ppermute | solution.py:27
  182.7 2.2 collective-permute-done.26
  194.9 10.4 %collective-permute-done.30 = bf16[128,1792]{1,0:T(8,128)(2,1)S(1)} collective-permute-done((bf16[128,1792]{1,0:T(8,128)(2,1)S(1)}, bf16[128,1792]{1,0:T(8,128)(2,1)S(1)}, u32[]{:S(2)}, u32[]{:S(2)}) %collective-permute-start.30) | collective-permute-done | bytes 458784 | tf_op jit(solution)/shard_map/ppermute | solution.py:22
  213.7 10.1 %collective-permute-done.33 = bf16[128,1792]{1,0:T(8,128)(2,1)S(1)} collective-permute-done((bf16[128,1792]{1,0:T(8,128)(2,1)S(1)}, bf16[128,1792]{1,0:T(8,128)(2,1)S(1)}, u32[]{:S(2)}, u32[]{:S(2)}) %collective-permute-start.33) | collective-permute-done | bytes 458784 | tf_op jit(solution)/shard_map/ppermute | solution.py:22
  (152 shorter events, 76.2 us)
Async XLA Ops:
  1.9 11.0 %collective-permute-start = (bf16[2,128,1792]{2,1,0:T(8,128)(2,1)S(1)}, bf16[2,128,1792]{2,1,0:T(8,128)(2,1)}, u32[]{:S(2)}, u32[]{:S(2)}) collective-permute-start(bf16[2,128,1792]{2,1,0:T(8,128)(2,1)S(1)} %pad_maximum_fusion.4), channel_id=1, source_target_pairs={{0,2},{2,0},{1,3},{3,1},{4,6},{6,4},{5,7},{7,5},{8,10},{10,8},{9,1... | collective-permute-start | bytes 2752520 | tf_op jit(solution)/shard_map/ppermute | solution.py:27
  2.4 23.6 %collective-permute-start.1 = (bf16[2,128,1792]{2,1,0:T(8,128)(2,1)S(1)}, bf16[2,128,1792]{2,1,0:T(8,128)(2,1)}, u32[]{:S(2)}, u32[]{:S(2)}) collective-permute-start(bf16[2,128,1792]{2,1,0:T(8,128)(2,1)S(1)} %pad_maximum_fusion.4), channel_id=1, source_target_pairs={{0,1},{1,0},{2,3},{3,2},{4,5},{5,4},{6,7},{7,6},{8,9},{9,8},{10,11... | collective-permute-start | bytes 2752520 | tf_op jit(solution)/shard_map/ppermute | solution.py:22
  38.7 4.9 %collective-permute-start.4 = (f32[5,1024]{1,0:T(8,128)S(1)}, f32[5,1024]{1,0:T(8,128)S(1)}, u32[]{:S(2)}, u32[]{:S(2)}) collective-permute-start(f32[5,1024]{1,0:T(8,128)S(1)} %pad_maximum_fusion.9), channel_id=1, source_target_pairs={{0,16},{8,24},{16,0},{24,8},{1,17},{9,25},{17,1},{25,9},{2,18},{10... | collective-permute-start | bytes 61448 | tf_op jit(solution)/shard_map/ppermute | solution.py:27
  49.9 22.1 %collective-permute-start.6 = (bf16[2,256,1024]{2,1,0:T(8,128)(2,1)S(1)}, bf16[2,256,1024]{2,1,0:T(8,128)(2,1)}, u32[]{:S(2)}, u32[]{:S(2)}) collective-permute-start(bf16[2,256,1024]{2,1,0:T(8,128)(2,1)S(1)} %pad_maximum_fusion.1), channel_id=1, source_target_pairs={{0,8},{8,0},{16,24},{24,16},{1,9},{9,1},{17,25},{25,17},{2,10},{10... | collective-permute-start | bytes 3145736 | tf_op jit(solution)/shard_map/ppermute | solution.py:27
  51.8 20.2 %collective-permute-start.7 = (bf16[2,256,1024]{2,1,0:T(8,128)(2,1)S(1)}, bf16[2,256,1024]{2,1,0:T(8,128)(2,1)}, u32[]{:S(2)}, u32[]{:S(2)}) collective-permute-start(bf16[2,256,1024]{2,1,0:T(8,128)(2,1)S(1)} %pad_maximum_fusion.1), channel_id=1, source_target_pairs={{8,16},{16,8},{9,17},{17,9},{10,18},{18,10},{11,19},{19,11},{12,20... | collective-permute-start | bytes 3145736 | tf_op jit(solution)/shard_map/ppermute | solution.py:174
  53.5 21.8 %collective-permute-start.8 = (bf16[2,256,1024]{2,1,0:T(8,128)(2,1)S(1)}, bf16[2,256,1024]{2,1,0:T(8,128)(2,1)}, u32[]{:S(2)}, u32[]{:S(2)}) collective-permute-start(bf16[2,256,1024]{2,1,0:T(8,128)(2,1)S(1)} %pad_maximum_fusion.1), channel_id=1, source_target_pairs={{0,4},{4,0},{1,5},{5,1},{2,6},{6,2},{3,7},{7,3},{8,12},{12,8},{9,1... | collective-permute-start | bytes 3145736 | tf_op jit(solution)/shard_map/ppermute | solution.py:27
  75.2 23.3 %collective-permute-start.10 = (bf16[2,256,1024]{2,1,0:T(8,128)(2,1)}, bf16[2,256,1024]{2,1,0:T(8,128)(2,1)}, u32[]{:S(2)}, u32[]{:S(2)}) collective-permute-start(bf16[2,256,1024]{2,1,0:T(8,128)(2,1)} %collective-permute-done.7), channel_id=1, source_target_pairs={{8,0},{16,24},{9,1},{17,25},{10,2},{18,26},{11,3},{19,27},{12,4},{... | collective-permute-start | bytes 3145736 | tf_op jit(solution)/shard_map/ppermute | solution.py:176
  76.5 22.0 %collective-permute-start.11 = (bf16[2,256,1024]{2,1,0:T(8,128)(2,1)}, bf16[2,256,1024]{2,1,0:T(8,128)(2,1)}, u32[]{:S(2)}, u32[]{:S(2)}) collective-permute-start(bf16[2,256,1024]{2,1,0:T(8,128)(2,1)} %collective-permute-done.6), channel_id=1, source_target_pairs={{0,4},{4,0},{1,5},{5,1},{2,6},{6,2},{3,7},{7,3},{8,12},{12,8},{9,1... | collective-permute-start | bytes 3145736 | tf_op jit(solution)/shard_map/ppermute | solution.py:27
  78.1 20.5 %collective-permute-start.9 = (bf16[2,256,1024]{2,1,0:T(8,128)(2,1)}, bf16[2,256,1024]{2,1,0:T(8,128)(2,1)}, u32[]{:S(2)}, u32[]{:S(2)}) collective-permute-start(bf16[2,256,1024]{2,1,0:T(8,128)(2,1)} %collective-permute-done.6), channel_id=1, source_target_pairs={{8,16},{16,8},{9,17},{17,9},{10,18},{18,10},{11,19},{19,11},{12,20... | collective-permute-start | bytes 3145736 | tf_op jit(solution)/shard_map/ppermute | solution.py:176
  98.6 24.7 %collective-permute-start.12 = (bf16[2,256,1024]{2,1,0:T(8,128)(2,1)}, bf16[2,256,1024]{2,1,0:T(8,128)(2,1)S(1)}, u32[]{:S(2)}, u32[]{:S(2)}) collective-permute-start(bf16[2,256,1024]{2,1,0:T(8,128)(2,1)} %collective-permute-done.9), channel_id=1, source_target_pairs={{8,0},{16,24},{9,1},{17,25},{10,2},{18,26},{11,3},{19,27},{12,4},{... | collective-permute-start | bytes 3145736 | tf_op jit(solution)/shard_map/ppermute | solution.py:179
  101.4 19.7 %collective-permute-start.13 = (bf16[2,256,1024]{2,1,0:T(8,128)(2,1)S(1)}, bf16[2,256,1024]{2,1,0:T(8,128)(2,1)S(1)}, u32[]{:S(2)}, u32[]{:S(2)}) collective-permute-start(bf16[2,256,1024]{2,1,0:T(8,128)(2,1)S(1)} %broadcast_select_fusion.1), channel_id=1, source_target_pairs={{0,4},{4,0},{1,5},{5,1},{2,6},{6,2},{3,7},{7,3},{8,12},{12,8},{9,1... | collective-permute-start | bytes 3145736 | tf_op jit(solution)/shard_map/ppermute | solution.py:27
  128.1 6.0 %collective-permute-start.16 = (f32[128,1536]{1,0:T(8,128)S(1)}, f32[128,1536]{1,0:T(8,128)S(1)}, u32[]{:S(2)}, u32[]{:S(2)}) collective-permute-start(f32[128,1536]{1,0:T(8,128)S(1)} %constant_dynamic-slice_fusion.7), channel_id=1, source_target_pairs={{0,2},{2,0},{1,3},{3,1},{4,6},{6,4},{5,7},{7,5},{8,10},{10,8},{9,1... | collective-permute-start | bytes 2359304 | tf_op jit(solution)/shard_map/ppermute | solution.py:27
  128.2 7.5 %collective-permute-start.18 = (f32[128,1536]{1,0:T(8,128)S(1)}, f32[128,1536]{1,0:T(8,128)S(1)}, u32[]{:S(2)}, u32[]{:S(2)}) collective-permute-start(f32[128,1536]{1,0:T(8,128)S(1)} %constant_dynamic-slice_fusion.6), channel_id=1, source_target_pairs={{0,2},{2,0},{1,3},{3,1},{4,6},{6,4},{5,7},{7,5},{8,10},{10,8},{9,1... | collective-permute-start | bytes 2359304 | tf_op jit(solution)/shard_map/ppermute | solution.py:27
  129.0 13.9 %collective-permute-start.14 = (bf16[2,128,1024]{2,1,0:T(8,128)(2,1)S(1)}, bf16[2,128,1024]{2,1,0:T(8,128)(2,1)S(1)}, u32[]{:S(2)}, u32[]{:S(2)}) collective-permute-start(bf16[2,128,1024]{2,1,0:T(8,128)(2,1)S(1)} %slice.208), channel_id=1, source_target_pairs={{0,4},{4,0},{1,5},{5,1},{2,6},{6,2},{3,7},{7,3},{8,12},{12,8},{9,1... | collective-permute-start | bytes 1572872 | tf_op jit(solution)/shard_map/ppermute | solution.py:27
  129.6 16.3 %collective-permute-start.15 = (bf16[2,128,1024]{2,1,0:T(8,128)(2,1)S(1)}, bf16[2,128,1024]{2,1,0:T(8,128)(2,1)S(1)}, u32[]{:S(2)}, u32[]{:S(2)}) collective-permute-start(bf16[2,128,1024]{2,1,0:T(8,128)(2,1)S(1)} %slice.166), channel_id=1, source_target_pairs={{0,8},{8,0},{16,24},{24,16},{1,9},{9,1},{17,25},{25,17},{2,10},{10... | collective-permute-start | bytes 1572872 | tf_op jit(solution)/shard_map/ppermute | solution.py:27
  134.2 11.6 %collective-permute-start.17 = (bf16[128,1536]{1,0:T(8,128)(2,1)S(1)}, bf16[128,1536]{1,0:T(8,128)(2,1)S(1)}, u32[]{:S(2)}, u32[]{:S(2)}) collective-permute-start(bf16[128,1536]{1,0:T(8,128)(2,1)S(1)} %fusion.24), channel_id=1, source_target_pairs={{0,1},{1,0},{2,3},{3,2},{4,5},{5,4},{6,7},{7,6},{8,9},{9,8},{10,11... | collective-permute-start | bytes 1179656 | tf_op jit(solution)/shard_map/ppermute | solution.py:22
  148.9 17.1 %collective-permute-start.21 = (bf16[128,2560]{1,0:T(8,128)(2,1)S(1)}, bf16[128,2560]{1,0:T(8,128)(2,1)S(1)}, u32[]{:S(2)}, u32[]{:S(2)}) collective-permute-start(bf16[128,2560]{1,0:T(8,128)(2,1)S(1)} %fusion.4), channel_id=1, source_target_pairs={{0,1},{1,0},{2,3},{3,2},{4,5},{5,4},{6,7},{7,6},{8,9},{9,8},{10,11... | collective-permute-start | bytes 1966088 | tf_op jit(solution)/shard_map/ppermute | solution.py:22
  166.3 4.3 %collective-permute-start.23 = (bf16[128,1536]{1,0:T(8,128)(2,1)S(1)}, bf16[128,1536]{1,0:T(8,128)(2,1)S(1)}, u32[]{:S(2)}, u32[]{:S(2)}) collective-permute-start(bf16[128,1536]{1,0:T(8,128)(2,1)S(1)} %add_convert_fusion.3), channel_id=1, source_target_pairs={{0,2},{2,0},{1,3},{3,1},{4,6},{6,4},{5,7},{7,5},{8,10},{10,8},{9,1... | collective-permute-start | bytes 1179656 | tf_op jit(solution)/shard_map/ppermute | solution.py:27
  176.4 4.7 %collective-permute-start.25 = (f32[4,1024]{1,0:T(4,128)S(1)}, f32[4,1024]{1,0:T(4,128)S(1)}, u32[]{:S(2)}, u32[]{:S(2)}) collective-permute-start(f32[4,1024]{1,0:T(4,128)S(1)} %fusion.43), channel_id=1, source_target_pairs={{0,16},{8,24},{16,0},{24,8},{1,17},{9,25},{17,1},{25,9},{2,18},{10... | collective-permute-start | bytes 49160 | tf_op jit(solution)/shard_map/ppermute | solution.py:27
  186.5 5.6 %collective-permute-start.27 = (f32[128,1792]{1,0:T(8,128)S(1)}, f32[128,1792]{1,0:T(8,128)S(1)}, u32[]{:S(2)}, u32[]{:S(2)}) collective-permute-start(f32[128,1792]{1,0:T(8,128)S(1)} %constant_dynamic-slice_fusion.3), channel_id=1, source_target_pairs={{0,2},{2,0},{1,3},{3,1},{4,6},{6,4},{5,7},{7,5},{8,10},{10,8},{9,1... | collective-permute-start | bytes 2752520 | tf_op jit(solution)/shard_map/ppermute | solution.py:27
  192.4 12.9 %collective-permute-start.30 = (bf16[128,1792]{1,0:T(8,128)(2,1)S(1)}, bf16[128,1792]{1,0:T(8,128)(2,1)S(1)}, u32[]{:S(2)}, u32[]{:S(2)}) collective-permute-start(bf16[128,1792]{1,0:T(8,128)(2,1)S(1)} %add_convert_fusion.2), channel_id=1, source_target_pairs={{0,1},{1,0},{2,3},{3,2},{4,5},{5,4},{6,7},{7,6},{8,9},{9,8},{10,11... | collective-permute-start | bytes 1376264 | tf_op jit(solution)/shard_map/ppermute | solution.py:22
  206.5 6.1 %collective-permute-start.32 = (f32[128,1792]{1,0:T(8,128)S(1)}, f32[128,1792]{1,0:T(8,128)S(1)}, u32[]{:S(2)}, u32[]{:S(2)}) collective-permute-start(f32[128,1792]{1,0:T(8,128)S(1)} %constant_dynamic-slice_fusion), channel_id=1, source_target_pairs={{0,2},{2,0},{1,3},{3,1},{4,6},{6,4},{5,7},{7,5},{8,10},{10,8},{9,1... | collective-permute-start | bytes 2752520 | tf_op jit(solution)/shard_map/ppermute | solution.py:27
  207.9 15.9 %collective-permute-start.31 = (f32[128,1792]{1,0:T(8,128)S(1)}, f32[128,1792]{1,0:T(8,128)S(1)}, u32[]{:S(2)}, u32[]{:S(2)}) collective-permute-start(f32[128,1792]{1,0:T(8,128)S(1)} %constant_dynamic-slice_fusion.1), channel_id=1, source_target_pairs={{0,2},{2,0},{1,3},{3,1},{4,6},{6,4},{5,7},{7,5},{8,10},{10,8},{9,1... | collective-permute-start | bytes 2752520 | tf_op jit(solution)/shard_map/ppermute | solution.py:27
  211.1 12.7 %collective-permute-start.33 = (bf16[128,1792]{1,0:T(8,128)(2,1)S(1)}, bf16[128,1792]{1,0:T(8,128)(2,1)S(1)}, u32[]{:S(2)}, u32[]{:S(2)}) collective-permute-start(bf16[128,1792]{1,0:T(8,128)(2,1)S(1)} %add_convert_fusion.1), channel_id=1, source_target_pairs={{0,1},{1,0},{2,3},{3,2},{4,5},{5,4},{6,7},{7,6},{8,9},{9,8},{10,11... | collective-permute-start | bytes 1376264 | tf_op jit(solution)/shard_map/ppermute | solution.py:22
  (23 other events, 142.4 us)
